TPU v7x, 32 devices: a whole 2x2x4 slice. The times are simulated.
32 devices in a mesh: dp: 8 (over z, x), patch: 4 (over y, core).
Axes of the slice: x: 2, y: 2, z: 4, core: 2. Of those that a mesh axis runs over, the one named last changes fastest.
Arguments:
- images: bfloat16 [192, 324, 512], P('dp', 'patch'), may hold values from -6 to 6
- cotangent: bfloat16 [192, 324, 512], P('dp', 'patch'), may hold values from -6 to 6
- res_class: int32 [192], P('dp'), may hold values from 0 to 2
- skip: int32 [192], P('dp'), may hold values 0 or 1
- ln_gain: float32 [512], replicated, may hold values from 0.5 to 1.5
- ln_bias: float32 [512], replicated, may hold values from -3 to 3
- w_in: bfloat16 [512, 3072], replicated, may hold values from -0.25 to 0.25
- b_in: float32 [3072], replicated, may hold values from -3 to 3
- gate_gain: float32 [1536], replicated, may hold values from 0.5 to 1.5
- gate_bias: float32 [1536], replicated, may hold values from -3 to 3
- w_spatial: bfloat16 [324, 324], replicated, may hold values from -0.3125 to 0.3125
- b_spatial: float32 [324], replicated, may hold values from -4 to 4
- w_out: bfloat16 [1536, 512], replicated, may hold values from -0.15625 to 0.15625
- b_out: float32 [512], replicated, may hold values from -3 to 3
Outputs:
- output: bfloat16 [192, 324, 512], P('dp', 'patch')
- grad_images: float32 [192, 324, 512], P('dp', 'patch')
- grad_ln_gain: float32 [512], replicated
- grad_ln_bias: float32 [512], replicated
- grad_w_in: float32 [512, 3072], replicated
- grad_b_in: float32 [3072], replicated
- grad_gate_gain: float32 [1536], replicated
- grad_gate_bias: float32 [1536], replicated
- grad_w_spatial: float32 [324, 324], replicated
- grad_b_spatial: float32 [324], replicated
- grad_w_out: float32 [1536, 512], replicated
- grad_b_out: float32 [512], replicated
All inputs are finite; a program needn't handle non-finite values. No bound on the sum of `skip` on one device may be relied on, other than what follows from the above.
Results may differ from a plain program's by a relative error of at most 0.0076.
Values may be sent and summed in bfloat16 or wider, within the bound.
A program may use at most 320 MiB of HBM per device.

v0:
```python
import jax
import jax.numpy as jnp
from jax import lax
from jax.sharding import PartitionSpec as P

SIDE_S = 10
SIDE_M = 14
SIDE_L = 18


epsilon = 1e-05


def slot_tables(slot_count, groups):
    total_slots = slot_count * groups
    slot_index = jnp.arange(total_slots, dtype=jnp.int32)
    block_of = slot_index // slot_count
    within = slot_index % slot_count
    target = jnp.arange(total_slots, dtype=jnp.int32)
    tables = []
    live_rows = []
    for side_len in (SIDE_S, SIDE_M, SIDE_L):
        per_group = side_len * side_len // groups
        is_live = within < per_group
        where_to = block_of * per_group + within
        tables.append(
            (is_live[:, None] & (where_to[:, None] == target[None, :])).astype(jnp.float32)
        )
        live_rows.append(is_live.astype(jnp.float32))
    return (jnp.stack(tables), jnp.stack(live_rows))


def layer_norm(values, gain_vec, shift_vec):
    centred = values - jnp.mean(values, axis=-1, keepdims=True)
    inv_std = lax.rsqrt(jnp.mean(centred * centred, axis=-1, keepdims=True) + epsilon)
    normed = centred * inv_std
    return (normed * gain_vec + shift_vec, normed, inv_std)


def norm_back(grad_out, normed, inv_std, gain_vec):
    grad_hat = grad_out * gain_vec
    return inv_std * (
        grad_hat
        - jnp.mean(grad_hat, axis=-1, keepdims=True)
        - normed * jnp.mean(grad_hat * normed, axis=-1, keepdims=True)
    )


def local(
    images,
    cotangent,
    res_class,
    skip,
    ln_gain,
    ln_bias,
    w_in,
    b_in,
    gate_gain,
    gate_bias,
    w_spatial,
    b_spatial,
    w_out,
    b_out,
):
    highest = lax.Precision.HIGHEST
    groups = lax.axis_size("patch")
    slot_count = images.shape[1]
    half_width = w_out.shape[0]
    my_index = lax.axis_index("patch")
    select_all, live_all = slot_tables(slot_count, groups)
    select_mine = lax.dynamic_slice_in_dim(select_all, my_index * slot_count, slot_count, 1)
    live_mine = lax.dynamic_slice_in_dim(live_all, my_index * slot_count, slot_count, 1)
    one_hot = (res_class[:, None] == jnp.arange(3, dtype=jnp.int32)[None, :]).astype(jnp.float32)
    keep_scale = (skip.astype(jnp.float32) / 0.9)[:, None] * jnp.einsum(
        "ic,cr->ir", one_hot, live_mine
    )
    spatial_full = w_spatial.astype(jnp.float32)
    picked = jnp.einsum("cra,ab->crb", select_mine, spatial_full, precision=highest)
    rows_class = jnp.einsum("crb,ctb->crt", picked, select_all, precision=highest)
    rows_image = jnp.einsum("ic,crt->irt", one_hot, rows_class, precision=highest).astype(
        jnp.bfloat16
    )
    bias_class = jnp.einsum("cra,a->cr", select_mine, b_spatial, precision=highest)
    bias_image = jnp.einsum("ic,cr->ir", one_hot, bias_class, precision=highest)
    inputs = images.astype(jnp.float32)
    normed_in, hat_in, inv_in = layer_norm(inputs, ln_gain, ln_bias)
    act_low = normed_in.astype(jnp.bfloat16)
    z_pre = jnp.einsum("ird,df->irf", act_low, w_in, preferred_element_type=jnp.float32) + b_in
    z_act, gelu_back = jax.vjp(jax.nn.gelu, z_pre)
    u_half = z_act[..., :half_width]
    v_half = z_act[..., half_width:]
    normed_gate, hat_gate, inv_gate = layer_norm(v_half, gate_gain, gate_bias)
    gate_low = normed_gate.astype(jnp.bfloat16)
    gate_all = lax.all_gather(gate_low, "patch", axis=1, tiled=True)
    spatial = (
        jnp.einsum("irt,itc->irc", rows_image, gate_all, preferred_element_type=jnp.float32)
        + bias_image[..., None]
    )
    gated_low = (u_half * spatial).astype(jnp.bfloat16)
    branch = jnp.einsum("irc,cd->ird", gated_low, w_out, preferred_element_type=jnp.float32) + b_out
    output = (inputs + keep_scale[..., None] * branch).astype(jnp.bfloat16)
    grad_in = cotangent.astype(jnp.float32)
    grad_branch = (grad_in * keep_scale[..., None]).astype(jnp.bfloat16)
    g_b_out = jnp.sum(grad_branch.astype(jnp.float32), axis=(0, 1))
    g_w_out = jnp.einsum("irc,ird->cd", gated_low, grad_branch, preferred_element_type=jnp.float32)
    grad_gated = jnp.einsum("ird,cd->irc", grad_branch, w_out, preferred_element_type=jnp.float32)
    grad_u = grad_gated * spatial
    grad_spatial = (grad_gated * u_half).astype(jnp.bfloat16)
    grad_bias_image = jnp.sum(grad_spatial.astype(jnp.float32), axis=2)
    grad_bias_class = jnp.einsum("ic,ir->cr", one_hot, grad_bias_image, precision=highest)
    g_b_spatial = jnp.einsum("cra,cr->a", select_mine, grad_bias_class, precision=highest)
    partial_gate = jnp.einsum(
        "irt,irc->itc", rows_image, grad_spatial, preferred_element_type=jnp.float32
    )
    grad_gate = lax.psum_scatter(partial_gate, "patch", scatter_dimension=1, tiled=True)
    grad_rows = jnp.einsum(
        "irc,itc->irt", grad_spatial, gate_all, preferred_element_type=jnp.float32
    )
    rows_class_grad = jnp.einsum("ic,irt->crt", one_hot, grad_rows, precision=highest)
    lifted = jnp.einsum("cra,crt->cat", select_mine, rows_class_grad, precision=highest)
    g_w_spatial = jnp.einsum("cat,ctb->ab", lifted, select_all, precision=highest)
    g_gate_gain = jnp.sum(grad_gate * hat_gate, axis=(0, 1))
    g_gate_bias = jnp.sum(grad_gate, axis=(0, 1))
    grad_v = norm_back(grad_gate, hat_gate, inv_gate, gate_gain)
    grad_z = jnp.concatenate([grad_u, grad_v], axis=-1)
    grad_pre = gelu_back(grad_z)[0].astype(jnp.bfloat16)
    g_b_in = jnp.sum(grad_pre.astype(jnp.float32), axis=(0, 1))
    g_w_in = jnp.einsum("ird,irf->df", act_low, grad_pre, preferred_element_type=jnp.float32)
    grad_act = jnp.einsum("irf,df->ird", grad_pre, w_in, preferred_element_type=jnp.float32)
    g_ln_gain = jnp.sum(grad_act * hat_in, axis=(0, 1))
    g_ln_bias = jnp.sum(grad_act, axis=(0, 1))
    grad_images = grad_in + norm_back(grad_act, hat_in, inv_in, ln_gain)
    summed = lax.psum(
        (
            g_ln_gain,
            g_ln_bias,
            g_w_in,
            g_b_in,
            g_gate_gain,
            g_gate_bias,
            g_w_spatial,
            g_b_spatial,
            g_w_out,
            g_b_out,
        ),
        ("dp", "patch"),
    )
    return (
        output,
        grad_images,
        summed[0],
        summed[1],
        summed[2],
        summed[3],
        summed[4],
        summed[5],
        summed[6],
        summed[7],
        summed[8],
        summed[9],
    )


def solution(mesh):
    placed = (
        P("dp", "patch", None),
        P("dp", "patch", None),
        P("dp"),
        P("dp"),
        P(),
        P(),
        P(),
        P(),
        P(),
        P(),
        P(),
        P(),
        P(),
        P(),
    )
    return jax.shard_map(
        local,
        mesh=mesh,
        in_specs=placed,
        out_specs=(
            P("dp", "patch", None),
            P("dp", "patch", None),
            P(),
            P(),
            P(),
            P(),
            P(),
            P(),
            P(),
            P(),
            P(),
            P(),
        ),
        check_vma=False,
    )
```

profile of v0, /device:TPU:1, one launch (start us, length us, event | category | flops | bytes accessed | tf_op | source)
XLA Modules:
  0.0 959.4 jit_solution(4240610860344493531)
XLA Ops:
  8.5 2.2 convert_reduce_fusion.2
  10.7 2.7 fusion.25
  13.4 21.8 %multiply_multiply_fusion.2 = (f32[24,81,3072]{2,1,0:T(8,128)}, f32[24,81,3072]{2,1,0:T(8,128)}) fusion(f32[3072]{0:T(1024)} %param.21, bf16[512,3072]{1,0:T(8,128)(2,1)S(1)} %copy-done, f32[512]{0:T(512)} %param.19, f32[512]{0:T(512)} %param.18, f32[24,81]{1,0:T(8,128)S(1)} %add_rsqrt_fusion.1, f32[24,81]{1,0:T(8,128)S(1)} %broadcast_multiply_fusion.5, ...), kind=kOutput, calls=%fused_computation.11 | convolution fusion | flops 6175014912 | bytes 52944064 | tf_op jit(solution)/shard_map/ird,df->irf/dot_general | solution.py:88
  35.3 5.4 slice_reduce_fusion
  41.8 1.3 fusion.50
  43.9 2.6 convolution_convert_fusion
  47.4 17.5 %convert_reduce_fusion.1 = (f32[24,81]{1,0:T(8,128)}, bf16[24,81,1536]{2,1,0:T(8,128)(2,1)}, f32[24,81]{1,0:T(8,128)}, f32[24,81,1536]{2,1,0:T(8,128)}) fusion(f32[24,81,3072]{2,1,0:T(8,128)} %get-tuple-element.64, f32[24,81]{1,0:T(8,128)S(1)} %broadcast_multiply_fusion.2, bf16[1536,512]{1,0:T(8,128)(2,1)} %param.26, ...), kind=kOutput, calls=%fused_computation.16 | convolution fusion | flops 3081531392 | bytes 45398400 | tf_op jit(solution)/shard_map/ird,cd->irc/dot_general | solution.py:106
  64.9 20.6 %fusion.37 = f32[24,324,1536]{2,1,0:T(8,128)} fusion(bf16[24,81,1536]{2,1,0:T(8,128)(2,1)} %get-tuple-element.54, bf16[24,81,324]{2,0,1:T(8,128)(2,1)} %convolution_convert_fusion), kind=kOutput, calls=%fused_computation.65 | convolution fusion | flops 1934917632 | bytes 55007424 | tf_op jit(solution)/shard_map/irt,irc->itc/dot_general | solution.py:112
  85.5 40.0 %copy.38 = f32[24,324,1536]{2,0,1:T(8,128)} copy(f32[24,324,1536]{2,1,0:T(8,128)} %fusion.37) | data formatting | bytes 95551488 | tf_op jit(solution)/shard_map/irt,irc->itc/dot_general | solution.py:112
  126.3 328.6 %reduce-scatter.4.cloned.1.call-done = f32[24,81,1536]{2,0,1:T(8,128)} async-done(((f32[24,324,1536]{2,0,1:T(8,128)}), f32[24,81,1536]{2,0,1:T(8,128)}) %reduce-scatter.4.cloned.1.call-update) | async-done | bytes 11943952
  454.9 16.1 %multiply_reduce_fusion = (f32[1536]{0:T(1024)}, f32[24,81]{1,0:T(8,128)S(1)}, f32[24,81]{1,0:T(8,128)S(1)}) fusion(f32[24,81,1536]{2,0,1:T(8,128)} %reduce-scatter.4.cloned.1.call-done, f32[24,81]{1,0:T(8,128)S(1)} %add_rsqrt_fusion, f32[24,81]{1,0:T(8,128)S(1)} %broadcast_multiply_fusion.2, f32[24,81,3072]{2,1,0:T(8,128)} %get-tuple-element.64, f32[1536]{0:T(1024)} %param.22), kind=kLoop, calls=%fused_computation.17 | loop fusion | flops 23882448 | bytes 23931264 | tf_op jit(solution)/shard_map/reduce_sum | solution.py:122
  471.0 14.8 %subtract_multiply_fusion = (f32[24,81,1536]{2,1,0:T(8,128)}, bf16[24,81,1536]{2,1,0:T(8,128)(2,1)S(1)}) fusion(f32[24,81,1536]{2,0,1:T(8,128)S(1)} %copy-done.1, f32[24,81]{1,0:T(8,128)S(1)} %broadcast_multiply_fusion, f32[24,81]{1,0:T(8,128)S(1)} %broadcast_multiply_fusion.1, f32[1536]{0:T(1024)S(1)} %copy-done.15, f32[24,81]{1,0:T(8,128)S(1)} %add_rsqrt_fusion, ...), kind=kLoop, calls=%fused_computation.18 | loop fusion | flops 29859840 | bytes 41847168 | tf_op jit(solution)/shard_map/mul | solution.py:42
  485.8 4.6 copy.33
  491.0 147.7 %all-gather.2.cloned.1.call-done = bf16[24,324,1536]{2,0,1:T(8,128)(2,1)} async-done(((bf16[24,81,1536]{2,0,1:T(8,128)(2,1)}), bf16[24,324,1536]{2,0,1:T(8,128)(2,1)}) %all-gather.2.cloned.1.call-update) | async-done | bytes 23887888 | tf_op jit(solution)/shard_map/all_gather | solution.py:94
  638.7 22.7 %fusion.7 = f32[24,81,324]{2,1,0:T(8,128)} fusion(bf16[24,81,1536]{2,1,0:T(8,128)(2,1)} %get-tuple-element.54, bf16[24,324,1536]{2,0,1:T(8,128)(2,1)} %all-gather.2.cloned.1.call-done), kind=kOutput, calls=%fused_computation.12 | convolution fusion | flops 1934917632 | bytes 32379264 | tf_op jit(solution)/shard_map/irc,itc->irt/dot_general | solution.py:116
  661.4 3.2 fusion.32
  664.7 1.0 fusion.48
  665.7 2.3 convolution_bitcast_fusion.2
  668.0 36.4 %add_multiply_fusion = (f32[24,81,1536]{2,1,0:T(8,128)}, bf16[24,81,1536]{2,1,0:T(8,128)(2,1)}) fusion(f32[24,81,1536]{2,1,0:T(8,128)} %get-tuple-element.66, f32[24,81]{1,0:T(8,128)S(1)} %fusion.58, f32[24,81,3072]{2,1,0:T(8,128)} %get-tuple-element.64, bf16[24,324,1536]{2,0,1:T(8,128)(2,1)} %all-gather.2.cloned.1.call-done, ...), kind=kOutput, calls=%fused_computation.27 | convolution fusion | flops 1946861568 | bytes 66959136 | tf_op jit(solution)/shard_map/irt,itc->irc/dot_general | solution.py:96
  704.4 24.7 %convert_reduce_fusion = (f32[3072]{0:T(1024)}, bf16[24,81,3072]{2,1,0:T(8,128)(2,1)S(1)}) fusion(f32[24,81,3072]{2,1,0:T(8,128)} %get-tuple-element.65, f32[3072]{0:T(1024)} %param.21, f32[24,81,1536]{2,1,0:T(8,128)} %get-tuple-element.57, f32[24,81,1536]{2,1,0:T(8,128)} %get-tuple-element.60), kind=kLoop, calls=%fused_computation.10 | loop fusion | flops 143324160 | bytes 59744256 | tf_op jit(solution)/shard_map/reduce_sum | solution.py:127
  729.2 11.1 %convolution_bitcast_fusion = f32[512,3072]{1,0:T(8,128)} fusion(bf16[24,81,3072]{2,1,0:T(8,128)(2,1)S(1)} %get-tuple-element.56, f32[512]{0:T(512)S(1)} %copy-done.26, f32[512]{0:T(512)S(1)} %copy-done.22, f32[24,81]{1,0:T(8,128)S(1)} %copy-done.13, f32[24,81]{1,0:T(8,128)S(1)} %copy-done.11, bf16[24,81,512]{2,0,1:T(8,128)(2,1)S(1)} %copy-done.2), kind=kOutput, calls=%fused_computation.41 | convolution fusion | flops 6121267200 | bytes 20245696 | tf_op jit(solution)/shard_map/ird,irf->df/dot_general | solution.py:128
  740.3 6.2 convolution_bitcast_fusion.1
  747.6 5.0 reduce_sum.147
  752.7 15.8 %fusion.24 = (f32[512]{0:T(512)S(1)}, f32[24,81]{1,0:T(8,128)S(1)}, f32[24,81]{1,0:T(8,128)S(1)}, f32[512]{0:T(512)S(1)}, f32[24,81,512]{2,1,0:T(8,128)S(1)}) fusion(f32[24,81]{1,0:T(8,128)S(1)} %copy-done.13, f32[24,81]{1,0:T(8,128)S(1)} %copy-done.11, bf16[24,81,512]{2,0,1:T(8,128)(2,1)} %param.14, f32[512]{0:T(512)} %param.18, ...), kind=kOutput, calls=%fused_computation.47 | convolution fusion | flops 6125243392 | bytes 21098880 | tf_op jit(solution)/shard_map/irf,df->ird/dot_general | solution.py:129
  768.6 4.0 convert_reduce_fusion.3
  772.6 4.2 copy.42
  776.9 7.7 fusion.27
  784.6 2.0 copy.41
  786.5 40.1 %all-reduce.1 = (f32[512]{0:T(512)}, f32[512]{0:T(512)}, f32[3072]{0:T(1024)}, f32[1536]{0:T(1024)}, f32[1536]{0:T(1024)}, /*index=5*/f32[324]{0:T(512)}, f32[512]{0:T(512)}) all-reduce(f32[512]{0:T(512)S(1)} %get-tuple-element.39, f32[512]{0:T(512)S(1)} %get-tuple-element.42, ...), channel_id=1, replica_groups=mesh['dp'=8,'patch'=4] {'dp','patch'}, use_global_device_ids=true, to_apply=%region_10.11 | all-reduce | flops 8004 | bytes 64032 | tf_op jit(solution)/shard_map/psum | solution.py:133
  826.6 117.2 %all-reduce.5.cloned.1.call-done = (f32[512,3072]{1,0:T(8,128)}, f32[324,324]{1,0:T(8,128)}, f32[1536,512]{1,0:T(8,128)}) async-done(((f32[512,3072]{1,0:T(8,128)}, f32[324,324]{1,0:T(8,128)}, f32[1536,512]{1,0:T(8,128)}), (f32[512,3072]{1,0:T(8,128)}, f32[324,324]{1,0:T(8,128)}, f32[1536,512]{1,0:T(8,128)})) %all-reduce.5.cloned.1.call-update) | async-done | bytes 9857104 | tf_op jit(solution)/shard_map/psum | solution.py:133
  943.8 6.4 copy.102
  951.0 1.7 copy.104
  (92 shorter events, 7.6 us)
Async XLA Ops:
  7.2 6.2 copy-start
  7.2 447.7 %reduce-scatter.4.cloned.1.call-start = ((), (), s32[]{:S(2)}) async-start(), calls=%async_computation.2 | async-start | bytes 59719680
  10.7 24.5 %copy-start.10 = (f32[24,81]{1,0:T(8,128)}, f32[24,81]{1,0:T(8,128)S(1)}, u32[]{:S(2)}) copy-start(f32[24,81]{1,0:T(8,128)S(1)} %broadcast_multiply_fusion.5) | copy-start | bytes 23332
  13.4 21.8 %copy-start.12 = (f32[24,81]{1,0:T(8,128)}, f32[24,81]{1,0:T(8,128)S(1)}, u32[]{:S(2)}) copy-start(f32[24,81]{1,0:T(8,128)S(1)} %add_rsqrt_fusion.1) | copy-start | bytes 23332
  35.3 5.4 copy-start.28
  35.3 8.7 copy-start.21
  47.4 17.5 %copy-start.17 = (f32[24,81]{1,0:T(8,128)}, f32[24,81]{1,0:T(8,128)S(1)}, u32[]{:S(2)}) copy-start(f32[24,81]{1,0:T(8,128)S(1)} %convolution_multiply_fusion) | copy-start | bytes 23332
  125.6 513.1 %all-gather.2.cloned.1.call-start = ((), (), s32[]{:S(2)}) async-start(), calls=%async_computation.1 | async-start | bytes 29859840 | tf_op jit(solution)/shard_map/all_gather | solution.py:94
  454.9 16.1 %copy-start.1 = (f32[24,81,1536]{2,0,1:T(8,128)S(1)}, f32[24,81,1536]{2,0,1:T(8,128)}, u32[]{:S(2)}) copy-start(f32[24,81,1536]{2,0,1:T(8,128)} %reduce-scatter.4.cloned.1.call-done) | copy-start | bytes 35831812
  454.9 16.1 %copy-start.15 = (f32[1536]{0:T(1024)S(1)}, f32[1536]{0:T(1024)}, u32[]{:S(2)}) copy-start(f32[1536]{0:T(1024)} %param.22) | copy-start | bytes 18436
  454.9 16.1 %copy-start.20 = (f32[1536]{0:T(1024)S(1)}, f32[1536]{0:T(1024)}, u32[]{:S(2)}) copy-start(f32[1536]{0:T(1024)} %param.23) | copy-start | bytes 18436
  485.8 4.6 copy-start.24
  490.4 453.4 %all-reduce.5.cloned.1.call-start = ((), (), s32[]{:S(2)}) async-start(), calls=%async_computation.3 | async-start | bytes 19881984 | tf_op jit(solution)/shard_map/psum | solution.py:133
  704.4 24.7 %copy-start.2 = (bf16[24,81,512]{2,0,1:T(8,128)(2,1)S(1)}, bf16[24,81,512]{2,0,1:T(8,128)(2,1)}, u32[]{:S(2)}) copy-start(bf16[24,81,512]{2,0,1:T(8,128)(2,1)} %param.14) | copy-start | bytes 5971972
  704.4 24.8 %copy-start.11 = (f32[24,81]{1,0:T(8,128)S(1)}, f32[24,81]{1,0:T(8,128)}, u32[]{:S(2)}) copy-start(f32[24,81]{1,0:T(8,128)} %copy-done.10) | copy-start | bytes 23332
  704.4 24.7 %copy-start.13 = (f32[24,81]{1,0:T(8,128)S(1)}, f32[24,81]{1,0:T(8,128)}, u32[]{:S(2)}) copy-start(f32[24,81]{1,0:T(8,128)} %copy-done.12) | copy-start | bytes 23332
  704.4 24.7 %copy-start.22 = (f32[512]{0:T(512)S(1)}, f32[512]{0:T(512)}, u32[]{:S(2)}) copy-start(f32[512]{0:T(512)} %param.18) | copy-start | bytes 6148
  704.4 24.7 %copy-start.26 = (f32[512]{0:T(512)S(1)}, f32[512]{0:T(512)}, u32[]{:S(2)}) copy-start(f32[512]{0:T(512)} %param.19) | copy-start | bytes 6148
  729.1 11.2 %copy-start.4 = (bf16[24,81,3072]{2,1,0:T(8,128)(2,1)}, bf16[24,81,3072]{2,1,0:T(8,128)(2,1)S(1)}, u32[]{:S(2)}) copy-start(bf16[24,81,3072]{2,1,0:T(8,128)(2,1)S(1)} %get-tuple-element.56) | copy-start | bytes 35831812
  729.1 11.1 %copy-start.5 = (bf16[24,81,1536]{2,1,0:T(8,128)(2,1)S(1)}, bf16[24,81,1536]{2,1,0:T(8,128)(2,1)}, u32[]{:S(2)}) copy-start(bf16[24,81,1536]{2,1,0:T(8,128)(2,1)} %get-tuple-element.61) | copy-start | bytes 17915908
  729.2 11.1 %copy-start.7 = (bf16[24,81,512]{2,0,1:T(8,128)(2,1)S(1)}, bf16[24,81,512]{2,0,1:T(8,128)(2,1)}, u32[]{:S(2)}) copy-start(bf16[24,81,512]{2,0,1:T(8,128)(2,1)} %param.15) | copy-start | bytes 5971972
  729.2 11.1 %copy-start.18 = (f32[24,81]{1,0:T(8,128)S(1)}, f32[24,81]{1,0:T(8,128)}, u32[]{:S(2)}) copy-start(f32[24,81]{1,0:T(8,128)} %copy-done.17) | copy-start | bytes 23332
  752.6 15.9 %copy-start.3 = (bf16[24,81,512]{2,0,1:T(8,128)(2,1)S(1)}, bf16[24,81,512]{2,0,1:T(8,128)(2,1)}, u32[]{:S(2)}) copy-start(bf16[24,81,512]{2,0,1:T(8,128)(2,1)} %param.14) | copy-start | bytes 5971972
  752.7 15.9 %copy-start.8 = (bf16[24,81,512]{2,0,1:T(8,128)(2,1)S(1)}, bf16[24,81,512]{2,0,1:T(8,128)(2,1)}, u32[]{:S(2)}) copy-start(bf16[24,81,512]{2,0,1:T(8,128)(2,1)} %param.15) | copy-start | bytes 5971972
  752.7 15.9 %copy-start.19 = (f32[24,81]{1,0:T(8,128)S(1)}, f32[24,81]{1,0:T(8,128)}, u32[]{:S(2)}) copy-start(f32[24,81]{1,0:T(8,128)} %copy-done.17) | copy-start | bytes 23332
  752.7 15.9 %copy-start.23 = (f32[512]{0:T(512)S(1)}, f32[512]{0:T(512)}, u32[]{:S(2)}) copy-start(f32[512]{0:T(512)} %param.18) | copy-start | bytes 6148
  772.6 4.3 copy-start.25
  772.6 4.3 copy-start.27
  776.9 9.6 %copy-start.14 = (f32[3072]{0:T(1024)S(1)}, f32[3072]{0:T(1024)}, u32[]{:S(2)}) copy-start(f32[3072]{0:T(1024)} %get-tuple-element.55) | copy-start | bytes 36868
  776.9 9.6 %copy-start.16 = (f32[1536]{0:T(1024)S(1)}, f32[1536]{0:T(1024)}, u32[]{:S(2)}) copy-start(f32[1536]{0:T(1024)} %get-tuple-element.36) | copy-start | bytes 18436
  943.8 6.4 copy-start.9
  943.8 7.2 copy-start.6
Sparse Core Ops, SparseCore 0:
  125.7 329.1 reduce-scatter.3
  490.5 148.1 all-gather.1
  746.6 197.1 all-reduce.4
where the time goes:
time: 970 us; the launch traced here: 959 us
  waiting for transfers between devices  593 us (61%)
  matrix products  174 us (18%)
  other arithmetic  77.9 us (8%)
  local copies, waits for them, and re-layouts  59.8 us (6%)
  blocking collectives  40.1 us (4%)
  between operations  14.5 us (1%)
    unnamed x4, waiting for transfers between devices  329 us
    all_gather x1, waiting for transfers between devices, local(): gate_all = lax.all_gather(gate_low, 'patch', axis=1, tiled=True)  148 us
    psum x1, waiting for transfers between devices, local(): lax.psum((g_ln_gain, g_ln_bias, g_w_in, g_b_in, g_gate_gain, g_gate_bias,...  117 us
    psum x1, blocking collectives, local(): lax.psum((g_ln_gain, g_ln_bias, g_w_in, g_b_in, g_gate_gain, g_gate_bias,...  40.1 us
    dot_general x1, local copies, waits for them, and re-layouts, local(): jnp.einsum('irt,irc->itc', rows_image, grad_spatial, preferred_element_ty...  40 us
    dot_general x1, matrix products, local(): jnp.einsum('irt,itc->irc', rows_image, gate_all, preferred_element_type=j...  36.4 us
    reduce_sum x1, other arithmetic, local(): g_b_in = jnp.sum(grad_pre.astype(jnp.float32), axis=(0, 1))  24.7 us
    dot_general x1, matrix products, local(): jnp.einsum('irc,itc->irt', grad_spatial, gate_all, preferred_element_type...  22.7 us
  transfers between devices with their start and end apart: 3, of which 3 were waited for; matrix products, arithmetic and copies ran while one was open for 4% of the time, Pallas kernels for 0%

commit v1 on v0

v1 whole, which is shorter than its diff:
```python
import functools

import jax
import jax.numpy as jnp
import numpy as np
from jax import lax
from jax.experimental import pallas as pl
from jax.experimental.pallas import tpu as pltpu
from jax.sharding import PartitionSpec as P

MESH = pl.DeviceIdType.MESH
SIDES = (10, 14, 18)
EPS = 1e-05
F32 = jnp.float32
BF16 = jnp.bfloat16
CT = 256
KEEP = np.float32(1.0) / np.float32(0.9)
GELU_C = np.float32(np.sqrt(2.0 / np.pi))
GELU_K = np.float32(0.044715)


def up(value, unit):
    return -(-value // unit) * unit


def dot(a, b):
    return lax.dot_general(a, b, (((1,), (0,)), ((), ())), preferred_element_type=F32)


def dot_nt(a, b):
    return lax.dot_general(a, b, (((1,), (1,)), ((), ())), preferred_element_type=F32)


def dot_tn(a, b):
    return lax.dot_general(a, b, (((0,), (0,)), ((), ())), preferred_element_type=F32)


def gelu_both(z):
    z2 = z * z
    t = jnp.tanh(z * (GELU_C + (GELU_C * GELU_K) * z2))
    a = 0.5 + 0.5 * t
    g = z * a
    slope = a + (g * (1.0 - t)) * (GELU_C + (3.0 * GELU_C * GELU_K) * z2)
    return g, slope


def fold(v):
    total = v[:, :128]
    for i in range(1, v.shape[1] // 128):
        total = total + v[:, i * 128 : (i + 1) * 128]
    return total


def col8(v):
    return jnp.sum(v.reshape(v.shape[0] // 8, 8, v.shape[1]), axis=0)


def position(j, device, groups):
    return jnp.where(lax.rem(j, 2) == 0, device, groups - 1 - device)


def pack_kernel(slot_count, groups, me_ref, order_ref, img_ref, cot_ref, *refs):
    outs, stage = refs[:groups], refs[groups]
    j = pl.program_id(0)
    me = me_ref[0]
    for k in range(groups):
        which = order_ref[j * groups + position(j, me ^ k, groups)]
        stage[0:slot_count, :] = img_ref[which].astype(F32)
        stage[slot_count : 2 * slot_count, :] = cot_ref[which].astype(F32)
        outs[k][0] = stage[...].astype(BF16)


def unpack_kernel(slot_count, groups, quarter, me_ref, rank_ref, key_ref, img_ref, cot_ref, *refs):
    backs, out_ref, grad_ref, stage = refs[:groups], refs[groups], refs[groups + 1], refs[groups + 2]
    i = pl.program_id(0)
    me = me_ref[0]
    key = key_ref[i]
    slot = rank_ref[i] // groups
    place = lax.rem(rank_ref[i], groups)
    owner = position(slot, place, groups)
    x = img_ref[0].astype(F32)
    dy = cot_ref[0].astype(F32)
    out_ref[0] = img_ref[0]
    grad_ref[0] = dy
    for k in range(groups):

        @pl.when((key > 0) & ((me ^ owner) == k))
        def _(k=k):
            stage[...] = backs[k][slot].astype(F32)
            live = jnp.where(key == 3, quarter[2], jnp.where(key == 2, quarter[1], quarter[0]))
            row = lax.broadcasted_iota(jnp.int32, (slot_count, 1), 0)
            mask = row < live
            out_ref[0] = (x + jnp.where(mask, stage[0:slot_count, :], 0.0)).astype(BF16)
            grad_ref[0] = dy + jnp.where(mask, stage[slot_count : 2 * slot_count, :], 0.0)


def image_work(q, slot_count, me, ins, outs, par, acc, scr):
    groups = len(ins)
    n = groups * q
    rows = up(n, 16)
    width = scr["xs"].shape[1]
    half = scr["gate"].shape[1]
    tiles = half // CT
    xs, dys, stage, act, dbr = scr["xs"], scr["dys"], scr["stage"], scr["act"], scr["dbr"]
    vs, gvp, gate, gated, dsp, dgs, dpre = (
        scr["vs"], scr["gvp"], scr["gate"], scr["gated"], scr["dsp"], scr["dgs"], scr["dpre"],
    )
    if rows > n:
        xs[rows - 16 : rows, :] = jnp.zeros((16, width), F32)
        dys[rows - 16 : rows, :] = jnp.zeros((16, width), F32)
    for m in range(groups):

        @pl.when(me == m)
        def _(m=m):
            for k in range(groups):
                at = (m ^ k) * q
                stage[...] = ins[k][0].astype(F32)
                xs[at : at + q, :] = stage[0:q, :]
                dys[at : at + q, :] = stage[slot_count : slot_count + q, :]

    x = xs[0:rows, :]
    mean = jnp.mean(x, axis=-1, keepdims=True)
    cen = x - mean
    inv = lax.rsqrt(jnp.mean(cen * cen, axis=-1, keepdims=True) + EPS)
    xhat = cen * inv
    xs[0:rows, :] = xhat
    scr["inv"][0:rows, :] = jnp.broadcast_to(inv, (rows, 128))
    act[0:rows, :] = (xhat * par["ln_gain"][...] + par["ln_bias"][...]).astype(BF16)
    db = (dys[0:rows, :] * KEEP).astype(BF16)
    dbr[0:rows, :] = db
    acc["b_out"][...] += col8(db.astype(F32))

    @pl.loop(0, tiles)
    def _(t):
        at = pl.ds(pl.multiple_of(t * CT, CT), CT)
        far = pl.ds(pl.multiple_of(half + t * CT, CT), CT)
        z = dot(act[0:rows, :], par["w_in"][:, far]) + par["b_in"][:, far]
        g, slope = gelu_both(z)
        vs[0:rows, at] = g
        gvp[0:rows, at] = slope.astype(BF16)

    total = fold(vs[0:rows, :])
    vmean = jnp.sum(total, axis=-1, keepdims=True) / half
    cen = vs[0:rows, :] - vmean
    vinv = lax.rsqrt(jnp.sum(fold(cen * cen), axis=-1, keepdims=True) / half + EPS)
    vhat = cen * vinv
    vs[0:rows, :] = vhat
    gate[0:rows, :] = (vhat * par["gate_gain"][...] + par["gate_bias"][...]).astype(BF16)
    if rows > n:
        tail = lax.broadcasted_iota(jnp.int32, (16, 1), 0) < n - (rows - 16)
        gate[rows - 16 : rows, :] = jnp.where(tail, gate[rows - 16 : rows, :].astype(F32), 0.0).astype(BF16)
    scr["hs"][0:rows, :] = jnp.zeros((rows, 128), F32)
    scr["hv"][0:rows, :] = jnp.zeros((rows, 128), F32)
    c = SIDES.index(int(round(np.sqrt(n))))

    @pl.loop(0, tiles)
    def _(t):
        at = pl.ds(pl.multiple_of(t * CT, CT), CT)
        z = dot(act[0:rows, :], par["w_in"][:, at]) + par["b_in"][:, at]
        u, slope = gelu_both(z)
        sp = dot(par["wsp"][c, 0:rows, 0:rows], gate[0:rows, at]) + par["bsp"][c, 0:rows, 0:1]
        gated[0:rows, at] = (u * sp).astype(BF16)
        dg = dot(dbr[0:rows, :], par["w_out_t"][:, at])
        pre = (dg * sp * slope).astype(BF16)
        dpre[0:rows, at] = pre
        acc["b_in"][:, at] += col8(pre.astype(F32))
        ds = (dg * u).astype(BF16)
        dsp[0:rows, at] = ds
        acc["b_sp"][0:rows, :] += fold(ds.astype(F32))
        dgate = dot(par["wsp_t"][c, 0:rows, 0:rows], ds)
        vh = vs[0:rows, at]
        acc["gate_bias"][:, at] += col8(dgate)
        acc["gate_gain"][:, at] += col8(dgate * vh)
        h = dgate * par["gate_gain"][:, at]
        dgs[0:rows, at] = h
        scr["hs"][0:rows, :] += fold(h)
        scr["hv"][0:rows, :] += fold(h * vh)

    hmean = jnp.sum(scr["hs"][0:rows, :], axis=-1, keepdims=True) / half
    hvmean = jnp.sum(scr["hv"][0:rows, :], axis=-1, keepdims=True) / half

    @pl.loop(0, tiles)
    def _(t):
        at = pl.ds(pl.multiple_of(t * CT, CT), CT)
        far = pl.ds(pl.multiple_of(half + t * CT, CT), CT)
        dv = vinv * (dgs[0:rows, at] - hmean - vs[0:rows, at] * hvmean)
        pre = (dv * gvp[0:rows, at].astype(F32)).astype(BF16)
        dpre[0:rows, far] = pre
        acc["b_in"][:, far] += col8(pre.astype(F32))

    acc["w_sp"][0:rows, 0:rows] += dot_nt(dsp[0:rows, :], gate[0:rows, :])
    branch = dot(gated[0:rows, :], par["w_out"][...]) + par["b_out"][...]
    dys[0:rows, :] = branch * KEEP
    dact = dot(dpre[0:rows, :], par["w_in_t"][...])
    xhat = xs[0:rows, :]
    acc["ln_bias"][...] += col8(dact)
    acc["ln_gain"][...] += col8(dact * xhat)
    h = dact * par["ln_gain"][...]
    back = scr["inv"][0:rows, 0:1] * (
        h - jnp.mean(h, axis=-1, keepdims=True) - xhat * jnp.mean(h * xhat, axis=-1, keepdims=True)
    )
    xs[0:rows, :] = back
    for m in range(groups):

        @pl.when(me == m)
        def _(m=m):
            for k in range(groups):
                at = (m ^ k) * q
                stage[0:q, :] = dys[at : at + q, :]
                stage[slot_count : slot_count + q, :] = xs[at : at + q, :]
                outs[k][0] = stage[...].astype(BF16)

    act_t = act[0:rows, :].T
    dbr_t = dbr[0:rows, :].T

    @pl.loop(0, 2 * tiles)
    def _(t):
        at = pl.ds(pl.multiple_of(t * CT, CT), CT)
        acc["w_in"][:, at] += dot(act_t, dpre[0:rows, at])

    @pl.loop(0, tiles)
    def _(t):
        at = pl.ds(pl.multiple_of(t * CT, CT), CT)
        acc["w_out_t"][:, at] += dot(dbr_t, gated[0:rows, at])


PAR = ("ln_gain", "ln_bias", "w_in", "w_in_t", "b_in", "gate_gain", "gate_bias", "wsp", "wsp_t", "bsp", "w_out", "w_out_t", "b_out")
ACC = ("w_in", "w_out_t", "w_sp", "b_in", "gate_gain", "gate_bias", "ln_gain", "ln_bias", "b_out", "b_sp")
SCR = ("stage", "xs", "dys", "inv", "act", "dbr", "vs", "gvp", "gate", "gated", "dsp", "dgs", "dpre", "hs", "hv")


def compute_kernel(slot_count, groups, quarter, me_ref, cls_ref, *refs):
    ins, refs = refs[:groups], refs[groups:]
    par, refs = dict(zip(PAR, refs)), refs[len(PAR) :]
    outs, refs = refs[:groups], refs[groups:]
    total_ref, refs = refs[0], refs[1:]
    acc, refs = dict(zip(ACC, refs)), refs[len(ACC) :]
    scr = dict(zip(SCR, refs))
    j = pl.program_id(0)
    me = me_ref[0]

    @pl.when(j == 0)
    def _():
        for ref in acc.values():
            ref[...] = jnp.zeros_like(ref)

    for c, q in enumerate(quarter):

        @pl.when(cls_ref[j] == c + 1)
        def _(q=q):
            image_work(q, slot_count, me, ins, outs, par, acc, scr)

    @pl.when(j == pl.num_programs(0) - 1)
    def _():
        width, wide = acc["w_in"].shape
        half = acc["w_out_t"].shape[1]
        total_ref[:, 0:wide] = acc["w_in"][...].astype(BF16)
        total_ref[:, wide : wide + half] = acc["w_out_t"][...].astype(BF16)
        base = wide + half
        side = acc["w_sp"].shape[0]
        total_ref[:, base:] = jnp.zeros((width, total_ref.shape[1] - base), BF16)
        span = acc["w_sp"].shape[1]
        total_ref[0:side, base : base + span] = acc["w_sp"][...].astype(BF16)
        sums = jnp.sum(acc["b_sp"][...], axis=-1, keepdims=True)
        total_ref[0:side, base + span : base + span + 128] = jnp.broadcast_to(sums, (side, 128)).astype(BF16)

        def line(name):
            return jnp.sum(acc[name][...], axis=0, keepdims=True)

        lines = []
        for name in ("b_in", "gate_gain", "gate_bias", "ln_gain", "ln_bias", "b_out"):
            v = line(name)
            lines += [v[:, i * width : (i + 1) * width] for i in range(v.shape[1] // width)]
        lines.append(jnp.zeros((16 - len(lines), width), F32))
        total_ref[side : side + 16, base : base + width] = jnp.concatenate(lines, axis=0).astype(BF16)


def reduce_plan(dp, patch, rows):
    dp_bits = [("dp", 1 << b) for b in range(dp.bit_length() - 1)]
    orders = [dp_bits[:1] + [("patch", 2)] + dp_bits[1:], [("patch", 2)] + dp_bits]
    plans = []
    for order in orders:
        size, steps = rows, []
        for axis, bit in order:
            halves = size // 2 >= 16
            steps.append((axis, bit, size, halves))
            size = size // 2 if halves else size
        plans.append(steps)
    return plans


def reduce_kernel(plans, pieces, g_ref, out_ref, acc, first, *refs):
    depth = len(plans[0])
    rbufs, (send_sem, recv_sem) = refs[:depth], refs[depth:]
    dp, patch = lax.axis_index("dp"), lax.axis_index("patch")
    core = patch & 1

    def peer(axis, bit):
        return (dp ^ bit, patch) if axis == "dp" else (dp, patch ^ bit)

    peers = [peer("patch", 1)] + [peer(a, b) for a, b, _, _ in plans[0]]
    barrier = pltpu.get_barrier_semaphore()
    for other in peers:
        pl.semaphore_signal(barrier, inc=1, device_id=other, device_id_type=MESH)
    pl.semaphore_wait(barrier, len(peers))

    rows, half = acc.shape
    cut = half // pieces
    mine = pl.multiple_of(core * half, 128)
    theirs = pl.multiple_of((1 - core) * half, 128)
    copies = []

    def send(src, dst, step, i, other):
        copy = pltpu.make_async_remote_copy(
            src_ref=src, dst_ref=dst, send_sem=send_sem.at[step, i], recv_sem=recv_sem.at[step, i],
            device_id=other, device_id_type=MESH,
        )
        copy.start()
        copies.append(copy)
        return copy

    def cols(i):
        return pl.ds(i * cut, cut)

    def shifted(base, i):
        return pl.ds(pl.multiple_of(base + i * cut, 128), cut)

    state = []
    flying = [
        send(g_ref.at[:, shifted(theirs, i)], first.at[:, cols(i)], 0, i, peer("patch", 1)) for i in range(pieces)
    ]
    for s in range(depth + 1):
        for i in range(pieces):
            plan = plans[i % 2]
            flying[i].wait_recv()
            if s == 0:
                lo = 0

                @pl.loop(0, rows, step=32)
                def _(r, i=i):
                    at = pl.ds(pl.multiple_of(r, 32), 32)
                    acc[at, cols(i)] = (
                        g_ref[at, shifted(mine, i)].astype(F32) + first[at, cols(i)].astype(F32)
                    ).astype(BF16)

                state.append(lo)
            else:
                axis, bit, size, halves = plan[s - 1]
                keep = size // 2 if halves else size
                lo = state[i]
                if not halves:
                    flying[i].wait_send()
                    copies[:] = [copy for copy in copies if copy is not flying[i]]
                unit = 16

                @pl.loop(0, keep, step=unit)
                def _(r, i=i, lo=lo, s=s):
                    at = pl.ds(pl.multiple_of(lo + r, unit), unit)
                    got = pl.ds(pl.multiple_of(r, unit), unit)
                    acc[at, cols(i)] = (
                        acc[at, cols(i)].astype(F32) + rbufs[s - 1][got, cols(i)].astype(F32)
                    ).astype(BF16)

            if s < depth:
                axis, bit, size, halves = plan[s]
                index = dp if axis == "dp" else patch
                up_half = jnp.where((index & bit) != 0, 1, 0)
                if halves:
                    keep = size // 2
                    give = pl.multiple_of(state[i] + (1 - up_half) * keep, 16)
                    state[i] = pl.multiple_of(state[i] + up_half * keep, 16)
                else:
                    keep, give = size, state[i]
                flying[i] = send(
                    acc.at[pl.ds(give, keep), cols(i)], rbufs[s].at[pl.ds(0, keep), cols(i)], s + 1, i, peer(axis, bit)
                )
    for i in range(pieces):
        axis, bit, size, halves = plans[i % 2][-1]
        keep = size // 2 if halves else size
        at = pl.ds(pl.multiple_of(state[i], 16), keep)
        out_ref[at, shifted(mine, i)] = acc[at, cols(i)]
    flying = [None] * pieces
    for s in range(depth, -1, -1):
        for i in range(pieces):
            if flying[i] is not None:
                flying[i].wait_recv()
                flying[i] = None
            step = 2 * depth + 1 - s
            if s == 0:
                at = pl.ds(0, rows)
                where = out_ref.at[at, shifted(mine, i)]
                flying[i] = send(where, where, step, i, peer("patch", 1))
            else:
                axis, bit, size, halves = plans[i % 2][s - 1]
                if not halves:
                    continue
                keep = size // 2
                index = dp if axis == "dp" else patch
                up_half = jnp.where((index & bit) != 0, 1, 0)
                where = out_ref.at[pl.ds(pl.multiple_of(state[i], 16), keep), shifted(mine, i)]
                flying[i] = send(where, where, step, i, peer(axis, bit))
                state[i] = state[i] - up_half * keep
    for i in range(pieces):
        flying[i].wait_recv()
    for copy in copies:
        copy.wait_send()


def all_reduce(total, dp, patch):
    rows, columns = total.shape
    plans = reduce_plan(dp, patch, rows)
    depth, half, pieces = len(plans[0]), columns // 2, 4
    sizes = [size // 2 if halves else size for _, _, size, halves in plans[0]]
    vmem = pl.BlockSpec(memory_space=pltpu.VMEM)
    return pl.pallas_call(
        functools.partial(reduce_kernel, plans, pieces),
        out_shape=jax.ShapeDtypeStruct(total.shape, total.dtype),
        in_specs=[vmem],
        out_specs=vmem,
        scratch_shapes=[pltpu.VMEM((rows, half), BF16), pltpu.VMEM((rows, half), BF16)]
        + [pltpu.VMEM((size, half), BF16) for size in sizes]
        + [pltpu.SemaphoreType.DMA((2 * depth + 2, pieces))] * 2,
        compiler_params=pltpu.CompilerParams(
            collective_id=1, has_side_effects=True, vmem_limit_bytes=40 * 1024 * 1024
        ),
        name="sum_gradients",
    )(total)


def local(images, cotangent, res_class, skip, ln_gain, ln_bias, w_in, b_in, gate_gain, gate_bias, w_spatial, b_spatial, w_out, b_out):
    groups = lax.axis_size("patch")
    dp = lax.axis_size("dp")
    count, slot_count, width = images.shape
    half = w_out.shape[0]
    wide = w_in.shape[1]
    slots = count // groups
    quarter = tuple(side * side // groups for side in SIDES)
    patches = groups * slot_count
    side = up(patches, 16)
    span = up(patches, 128)
    stage_rows = up(2 * slot_count, 16)
    me = lax.axis_index("patch").astype(jnp.int32)

    key = jnp.where(skip != 0, res_class + 1, 0).astype(jnp.int32)
    index = jnp.arange(count, dtype=jnp.int32)
    before = (key[None, :] > key[:, None]) | ((key[None, :] == key[:, None]) & (index[None, :] < index[:, None]))
    rank = jnp.sum(before.astype(jnp.int32), axis=1)
    hit = rank[None, :] == index[:, None]
    order = jnp.sum(jnp.where(hit, index[None, :], 0), axis=1)
    sorted_key = jnp.sum(jnp.where(hit, key[None, :], 0), axis=1)
    slot_index = jnp.arange(slots, dtype=jnp.int32)
    spot = slot_index * groups + jnp.where(slot_index % 2 == 0, me, groups - 1 - me)
    cls = jnp.sum(jnp.where(spot[:, None] == index[None, :], sorted_key[None, :], 0), axis=1)
    me1 = me.reshape(1)

    whole = pl.BlockSpec(memory_space=pltpu.VMEM)
    block = pl.BlockSpec((1, stage_rows, width), lambda j, *_: (j, 0, 0))
    parcel = jax.ShapeDtypeStruct((slots, stage_rows, width), BF16)
    packed = pl.pallas_call(
        functools.partial(pack_kernel, slot_count, groups),
        out_shape=[parcel] * groups,
        grid_spec=pltpu.PrefetchScalarGridSpec(
            num_scalar_prefetch=2, grid=(slots,), in_specs=[whole, whole], out_specs=[block] * groups,
            scratch_shapes=[pltpu.VMEM((stage_rows, width), F32)],
        ),
        name="pack",
    )(me1, order, images, cotangent)

    def swap(parts):
        return [parts[0]] + [
            lax.ppermute(parts[k], "patch", [(i, i ^ k) for i in range(groups)]) for k in range(1, groups)
        ]

    arrived = swap(packed)

    row = jnp.arange(side, dtype=jnp.int32)
    w_pad = jnp.pad(w_spatial, ((0, side - patches), (0, side - patches)))
    b_pad = jnp.pad(b_spatial, (0, side - patches))
    masks = [(row < groups * q) for q in quarter]
    wsp = jnp.stack([jnp.where(m[:, None] & m[None, :], w_pad, 0) for m in masks]).astype(BF16)
    wsp_t = jnp.swapaxes(wsp, 1, 2)
    bsp = jnp.stack([jnp.broadcast_to(jnp.where(m, b_pad, 0.0)[:, None], (side, 128)) for m in masks])
    par = {
        "ln_gain": ln_gain[None, :], "ln_bias": ln_bias[None, :], "w_in": w_in, "w_in_t": w_in.T, "b_in": b_in[None, :],
        "gate_gain": gate_gain[None, :], "gate_bias": gate_bias[None, :], "wsp": wsp, "wsp_t": wsp_t, "bsp": bsp,
        "w_out": w_out, "w_out_t": w_out.T, "b_out": b_out[None, :],
    }
    acc = {
        "w_in": (width, wide), "w_out_t": (width, half), "w_sp": (side, span), "b_in": (8, wide), "gate_gain": (8, half),
        "gate_bias": (8, half), "ln_gain": (8, width), "ln_bias": (8, width), "b_out": (8, width), "b_sp": (side, 128),
    }
    scr = {
        "stage": ((stage_rows, width), F32), "xs": ((side, width), F32), "dys": ((side, width), F32),
        "inv": ((side, 128), F32), "act": ((side, width), BF16), "dbr": ((side, width), BF16), "vs": ((side, half), F32),
        "gvp": ((side, half), BF16), "gate": ((side, half), BF16), "gated": ((side, half), BF16), "dsp": ((side, half), BF16),
        "dgs": ((side, half), F32), "dpre": ((side, wide), BF16), "hs": ((side, 128), F32), "hv": ((side, 128), F32),
    }
    columns = wide + half + 512
    results = pl.pallas_call(
        functools.partial(compute_kernel, slot_count, groups, quarter),
        out_shape=[parcel] * groups + [jax.ShapeDtypeStruct((width, columns), BF16)],
        grid_spec=pltpu.PrefetchScalarGridSpec(
            num_scalar_prefetch=2, grid=(slots,), in_specs=[block] * groups + [whole] * len(PAR),
            out_specs=[block] * groups + [whole],
            scratch_shapes=[pltpu.VMEM(acc[name], F32) for name in ACC] + [pltpu.VMEM(*scr[name]) for name in SCR],
        ),
        compiler_params=pltpu.CompilerParams(vmem_limit_bytes=60 * 1024 * 1024),
        name="images",
    )(me1, cls, *arrived, *[par[name] for name in PAR])
    returned = swap(results[:groups])
    summed = all_reduce(results[groups], dp, groups)

    own = pl.BlockSpec((1, slot_count, width), lambda i, *_: (i, 0, 0))
    output, grad_images = pl.pallas_call(
        functools.partial(unpack_kernel, slot_count, groups, quarter),
        out_shape=[jax.ShapeDtypeStruct(images.shape, BF16), jax.ShapeDtypeStruct(images.shape, F32)],
        grid_spec=pltpu.PrefetchScalarGridSpec(
            num_scalar_prefetch=3, grid=(count,), in_specs=[own, own] + [whole] * groups, out_specs=[own, own],
            scratch_shapes=[pltpu.VMEM((stage_rows, width), F32)],
        ),
        name="unpack",
    )(me1, rank, key, images, cotangent, *returned)

    base = wide + half
    small = summed[:, base:].astype(F32)
    lines = small[side : side + 16].reshape(-1)
    ends = np.cumsum([0, wide, half, half, width, width, width])
    g_b_in, g_gate_gain, g_gate_bias, g_ln_gain, g_ln_bias, g_b_out = [
        lines[ends[i] : ends[i + 1]] for i in range(6)
    ]
    return (
        output, grad_images, g_ln_gain, g_ln_bias, summed[:, :wide].astype(F32), g_b_in, g_gate_gain, g_gate_bias,
        small[:patches, :patches], small[:patches, span], summed[:, wide:base].T.astype(F32), g_b_out,
    )


def solution(mesh):
    placed = (P("dp", "patch", None),) * 2 + (P("dp"),) * 2 + (P(),) * 10
    return jax.shard_map(
        local, mesh=mesh, in_specs=placed, out_specs=(P("dp", "patch", None),) * 2 + (P(),) * 10, check_vma=False,
    )
```

time: 970 us -> 320 us (0.33)
  waiting for transfers between devices: 593 us -> 69.2 us
  Pallas kernels: 0 us -> 195 us
  matrix products: 174 us -> 0 us
  other arithmetic: 77.9 us -> 10.5 us
  blocking collectives: 40.1 us -> 0 us
  local copies, waits for them, and re-layouts: 59.8 us -> 36.8 us
  between operations: 14.5 us -> 0.79 us
    unnamed x4 -> x0, waiting for transfers between devices: 329 us -> none
    pallas_call x0 -> x4, Pallas kernels: none -> 195 us  [the longest x1 88.9 us: all_reduce(): pl.pallas_call(functools.partial(reduce_kernel, plans, pieces), out_shape...]
    dot_general x20 -> x0, matrix products: 174 us -> none  [the longest x1 36.4 us: local(): jnp.einsum('irt,itc->irc', rows_image, gate_all, preferred_element_type=j...]
    all_gather x1 -> x0, waiting for transfers between devices: 148 us -> none  [local(): gate_all = lax.all_gather(gate_low, 'patch', axis=1, tiled=True)]
    psum x1 -> x0, waiting for transfers between devices: 117 us -> none  [local(): lax.psum((g_ln_gain, g_ln_bias, g_w_in, g_b_in, g_gate_gain, g_gate_bias,...]
    ppermute x0 -> x6, waiting for transfers between devices: none -> 69.2 us  [swap(): lax.ppermute(parts[k], 'patch', [(i, i ^ k) for i in range(groups)])]
    reduce_sum x7 -> x3, other arithmetic: 60.1 us -> 1.5 us  [the longest x1 0.69 us: local(): jnp.sum(jnp.where(spot[:, None] == index[None, :], sorted_key[None, :], 0...]
    psum x1 -> x0, blocking collectives: 40.1 us -> none  [local(): lax.psum((g_ln_gain, g_ln_bias, g_w_in, g_b_in, g_gate_gain, g_gate_bias,...]
  transfers between devices with their start and end apart: 3 -> 6, of which waited for: 3 -> 4; matrix products, arithmetic and copies ran while one was open for 4% -> 8% of each run, Pallas kernels for 0% -> 0%
where the time goes in v1:
time: 320 us; the launch traced here: 318 us
  Pallas kernels  195 us (61%)
  waiting for transfers between devices  69.2 us (22%)
  local copies, waits for them, and re-layouts  36.8 us (11%)
  other arithmetic  10.5 us (3%)
  starting transfers between devices  4.94 us (2%)
    pallas_call x1, Pallas kernels, all_reduce(): pl.pallas_call(functools.partial(reduce_kernel, plans, pieces), out_shape...  88.9 us
    pallas_call x1, Pallas kernels, local(): pl.pallas_call(functools.partial(compute_kernel, slot_count, groups, quar...  82.9 us
    ppermute x6, waiting for transfers between devices, swap(): lax.ppermute(parts[k], 'patch', [(i, i ^ k) for i in range(groups)])  69.2 us
    unnamed x30, local copies, waits for them, and re-layouts  28 us
    pallas_call x1, Pallas kernels, local(): pl.pallas_call(functools.partial(unpack_kernel, slot_count, groups, quart...  17.6 us
  transfers between devices with their start and end apart: 6, of which 4 were waited for; matrix products, arithmetic and copies ran while one was open for 8% of the time, Pallas kernels for 0%

profile of v1, /device:TPU:1, one launch (start us, length us, event | category | flops | bytes accessed | tf_op | source)
XLA Modules:
  0.0 317.8 jit_solution(2164431401284789636)
XLA Ops:
  0.6 0.7 compare_select_fusion.1.key_ref
  1.5 0.6 select_reduce_fusion
  2.1 3.7 %copy.54.img_ref = bf16[24,81,512]{2,1,0:T(8,128)(2,1)} copy(bf16[24,81,512]{2,0,1:T(8,128)(2,1)} %param.14) | data formatting | bytes 3981312 | tf_op args[0]
  5.9 2.1 copy.55.cot_ref
  7.9 6.1 %pack.1 = (bf16[6,176,512]{2,1,0:T(8,128)(2,1)}, bf16[6,176,512]{2,1,0:T(8,128)(2,1)}, bf16[6,176,512]{2,1,0:T(8,128)(2,1)}, bf16[6,176,512]{2,1,0:T(8,128)(2,1)}) custom-call(s32[1]{0:T(128)} %bitcast.me_ref, s32[24]{0:T(128)} %get-tuple-element.70.order_ref, bf16[24,81,512]{2,1,0:T(8,128)(2,1)} %copy.54.img_ref, bf16[24,81,512]{2,1,0:T(8,128)(2,1)} %copy.55.cot_ref), custom_call_target="tpu_custom_call" | custom-call | tf_op jit(solution)/shard_map/pack/pallas_call | solution.py:459
  14.1 2.7 collective-permute-start.1
  16.8 0.6 broadcast_in_dim.96.refs_9_
  18.5 1.3 fusion.6
  19.8 2.5 copy.53.refs_11_
  22.3 2.6 copy.52
  24.9 2.8 copy.50
  27.7 0.7 select_reduce_fusion.2.cls_ref
  28.7 0.9 pad_maximum_fusion.1.refs_13_
  29.5 11.7 %collective-permute-done.1.refs_2_ = bf16[6,176,512]{2,1,0:T(8,128)(2,1)} collective-permute-done((bf16[6,176,512]{2,1,0:T(8,128)(2,1)}, bf16[6,176,512]{2,1,0:T(8,128)(2,1)}, u32[]{:S(2)}, u32[]{:S(2)}) %collective-permute-start.1) | collective-permute-done | bytes 1081376 | tf_op jit(solution)/shard_map/ppermute | solution.py:471
  41.3 23.2 %collective-permute-done.2.refs_3_ = bf16[6,176,512]{2,1,0:T(8,128)(2,1)} collective-permute-done((bf16[6,176,512]{2,1,0:T(8,128)(2,1)}, bf16[6,176,512]{2,1,0:T(8,128)(2,1)}, u32[]{:S(2)}, u32[]{:S(2)}) %collective-permute-start.2) | collective-permute-done | bytes 1081376 | tf_op jit(solution)/shard_map/ppermute | solution.py:471
  64.4 82.9 %images.1 = (bf16[6,176,512]{2,1,0:T(8,128)(2,1)}, bf16[6,176,512]{2,1,0:T(8,128)(2,1)}, bf16[6,176,512]{2,1,0:T(8,128)(2,1)}, bf16[6,176,512]{2,1,0:T(8,128)(2,1)}, bf16[512,5120]{1,0:T(8,128)(2,1)}) custom-call(s32[1]{0:T(128)} %bitcast.me_ref, s32[6]{0:T(128)} %select_reduce_fusion.2.cls_ref, bf16[6,176,512]{2,1,0:T(8,128)(2,1)} %get-tuple-element.23.refs_0_, ...), custom_call_target="tpu_custom_call" | custom-call | tf_op jit(solution)/shard_map/images/pallas_call | solution.py:499
  147.4 2.5 copy-done.1
  149.9 88.9 %sum_gradients.1 = bf16[512,5120]{1,0:T(8,128)(2,1)S(1)} custom-call(bf16[512,5120]{1,0:T(8,128)(2,1)S(1)} %copy-done.1), custom_call_target="tpu_custom_call" | custom-call | tf_op jit(solution)/shard_map/sum_gradients/pallas_call | solution.py:415
  239.2 1.8 copy-done
  241.4 1.8 collective-permute-start.5
  243.8 0.8 slice.80
  244.6 0.6 slice.65
  245.2 0.6 slice.69
  245.8 0.6 slice.67
  246.4 2.4 copy.58
  248.8 1.6 slice_reduce_fusion
  250.4 5.4 %slice_convert_fusion = f32[512,3072]{1,0:T(8,128)} fusion(bf16[512,5120]{1,0:T(8,128)(2,1)} %copy-done), kind=kLoop, calls=%fused_computation.1 | loop fusion | flops 1572864 | bytes 9437184 | tf_op jit(solution)/shard_map/convert_element_type | solution.py:532
  255.8 10.6 %collective-permute-done.4.refs_2_ = bf16[6,176,512]{2,1,0:T(8,128)(2,1)} collective-permute-done((bf16[6,176,512]{2,1,0:T(8,128)(2,1)}, bf16[6,176,512]{2,1,0:T(8,128)(2,1)}, u32[]{:S(2)}, u32[]{:S(2)}) %collective-permute-start.4) | collective-permute-done | bytes 1081376 | tf_op jit(solution)/shard_map/ppermute | solution.py:471
  266.4 23.8 %collective-permute-done.5.refs_3_ = bf16[6,176,512]{2,1,0:T(8,128)(2,1)} collective-permute-done((bf16[6,176,512]{2,1,0:T(8,128)(2,1)}, bf16[6,176,512]{2,1,0:T(8,128)(2,1)}, u32[]{:S(2)}, u32[]{:S(2)}) %collective-permute-start.5) | collective-permute-done | bytes 1081376 | tf_op jit(solution)/shard_map/ppermute | solution.py:471
  290.2 17.6 %unpack.1 = (bf16[24,81,512]{2,1,0:T(8,128)(2,1)}, f32[24,81,512]{2,1,0:T(8,128)}) custom-call(s32[1]{0:T(128)} %bitcast.me_ref, s32[24]{0:T(128)} %copy-done.9, s32[24]{0:T(128)} %copy-done.8, bf16[24,81,512]{2,1,0:T(8,128)(2,1)} %copy.54.img_ref, bf16[24,81,512]{2,1,0:T(8,128)(2,1)} %copy.55.cot_ref, bf16[6,176,512]{2,1,0:T(8,128)(2,1)} %get-tuple-element.27.refs_0_, ...), custom_call_target="tpu_custom_call" | custom-call | tf_op jit(solution)/shard_map/unpack/pallas_call | solution.py:514
  307.8 3.5 %copy.56 = bf16[24,81,512]{2,0,1:T(8,128)(2,1)} copy(bf16[24,81,512]{2,1,0:T(8,128)(2,1)} %get-tuple-element.58) | data formatting | bytes 3981312
  311.3 6.5 %copy.57 = f32[24,81,512]{2,0,1:T(8,128)} copy(f32[24,81,512]{2,1,0:T(8,128)} %get-tuple-element.59) | data formatting | bytes 7962624
  (42 shorter events, 3.1 us)
Async XLA Ops:
  1.3 4.5 %copy-start.8 = (s32[24]{0:T(128)}, s32[24]{0:T(128)S(1)}, u32[]{:S(2)}) copy-start(s32[24]{0:T(128)S(1)} %compare_select_fusion.1.key_ref) | copy-start | bytes 292
  1.5 4.3 %copy-start.9 = (s32[24]{0:T(128)}, s32[24]{0:T(128)S(1)}, u32[]{:S(2)}) copy-start(s32[24]{0:T(128)S(1)} %convert_reduce_fusion.rank_ref) | copy-start | bytes 292
  2.1 3.7 %copy-start.4 = (bf16[24,81,512]{2,0,1:T(8,128)(2,1)S(1)}, bf16[24,81,512]{2,0,1:T(8,128)(2,1)}, u32[]{:S(2)}) copy-start(bf16[24,81,512]{2,0,1:T(8,128)(2,1)} %param.15) | copy-start | bytes 5971972
  7.9 8.9 %copy-start.6 = (f32[1536]{0:T(1024)S(1)}, f32[1536]{0:T(1024)}, u32[]{:S(2)}) copy-start(f32[1536]{0:T(1024)} %param.22) | copy-start | bytes 18436
  7.9 9.5 %copy-start.7 = (f32[1536]{0:T(1024)S(1)}, f32[1536]{0:T(1024)}, u32[]{:S(2)}) copy-start(f32[1536]{0:T(1024)} %param.23) | copy-start | bytes 18436
  7.9 10.1 %copy-start.5 = (bf16[324,324]{1,0:T(8,128)(2,1)S(1)}, bf16[324,324]{1,0:T(8,128)(2,1)}, u32[]{:S(2)}) copy-start(bf16[324,324]{1,0:T(8,128)(2,1)} %param.24) | copy-start | bytes 629860
  14.0 15.6 %collective-permute-start = (bf16[6,176,512]{2,1,0:T(8,128)(2,1)}, bf16[6,176,512]{2,1,0:T(8,128)(2,1)}, u32[]{:S(2)}, u32[]{:S(2)}) collective-permute-start(bf16[6,176,512]{2,1,0:T(8,128)(2,1)} %get-tuple-element.24), channel_id=1, source_target_pairs={{0,1},{1,0},{2,3},{3,2},{4,5},{5,4},{6,7},{7,6},{8,9},{9,8},{10,11... | collective-permute-start | bytes 3244040 | tf_op jit(solution)/shard_map/ppermute | solution.py:471
  14.1 27.2 %collective-permute-start.1 = (bf16[6,176,512]{2,1,0:T(8,128)(2,1)}, bf16[6,176,512]{2,1,0:T(8,128)(2,1)}, u32[]{:S(2)}, u32[]{:S(2)}) collective-permute-start(bf16[6,176,512]{2,1,0:T(8,128)(2,1)} %get-tuple-element.25), channel_id=1, source_target_pairs={{0,2},{1,3},{2,0},{3,1},{4,6},{5,7},{6,4},{7,5},{8,10},{9,11},{10,... | collective-permute-start | bytes 3244040 | tf_op jit(solution)/shard_map/ppermute | solution.py:471
  16.8 47.7 %collective-permute-start.2 = (bf16[6,176,512]{2,1,0:T(8,128)(2,1)}, bf16[6,176,512]{2,1,0:T(8,128)(2,1)}, u32[]{:S(2)}, u32[]{:S(2)}) collective-permute-start(bf16[6,176,512]{2,1,0:T(8,128)(2,1)} %get-tuple-element.26), channel_id=1, source_target_pairs={{0,3},{1,2},{2,1},{3,0},{4,7},{5,6},{6,5},{7,4},{8,11},{9,10},{10,... | collective-permute-start | bytes 3244040 | tf_op jit(solution)/shard_map/ppermute | solution.py:471
  19.8 5.1 %copy-start.2 = (bf16[512,3072]{1,0:T(8,128)(2,1)S(1)}, bf16[512,3072]{1,0:T(8,128)(2,1)}, u32[]{:S(2)}) copy-start(bf16[512,3072]{1,0:T(8,128)(2,1)} %refs_6_.1) | copy-start | bytes 9437188
  24.9 2.8 copy-start.10
  147.4 2.5 copy-start.1
  238.7 2.3 copy-start
  238.9 5.0 %copy-start.3 = (f32[512,512]{1,0:T(8,128)}, f32[512,512]{1,0:T(8,128)S(1)}, u32[]{:S(2)}) copy-start(f32[512,512]{1,0:T(8,128)S(1)} %slice_convert_fusion.1) | copy-start | bytes 3145732
  241.0 14.8 %collective-permute-start.3 = (bf16[6,176,512]{2,1,0:T(8,128)(2,1)}, bf16[6,176,512]{2,1,0:T(8,128)(2,1)}, u32[]{:S(2)}, u32[]{:S(2)}) collective-permute-start(bf16[6,176,512]{2,1,0:T(8,128)(2,1)} %get-tuple-element.28), channel_id=1, source_target_pairs={{0,1},{1,0},{2,3},{3,2},{4,5},{5,4},{6,7},{7,6},{8,9},{9,8},{10,11... | collective-permute-start | bytes 3244040 | tf_op jit(solution)/shard_map/ppermute | solution.py:471
  241.1 25.3 %collective-permute-start.4 = (bf16[6,176,512]{2,1,0:T(8,128)(2,1)}, bf16[6,176,512]{2,1,0:T(8,128)(2,1)}, u32[]{:S(2)}, u32[]{:S(2)}) collective-permute-start(bf16[6,176,512]{2,1,0:T(8,128)(2,1)} %get-tuple-element.29), channel_id=1, source_target_pairs={{0,2},{1,3},{2,0},{3,1},{4,6},{5,7},{6,4},{7,5},{8,10},{9,11},{10,... | collective-permute-start | bytes 3244040 | tf_op jit(solution)/shard_map/ppermute | solution.py:471
  241.4 48.8 %collective-permute-start.5 = (bf16[6,176,512]{2,1,0:T(8,128)(2,1)}, bf16[6,176,512]{2,1,0:T(8,128)(2,1)}, u32[]{:S(2)}, u32[]{:S(2)}) collective-permute-start(bf16[6,176,512]{2,1,0:T(8,128)(2,1)} %get-tuple-element.30), channel_id=1, source_target_pairs={{0,3},{1,2},{2,1},{3,0},{4,7},{5,6},{6,5},{7,4},{8,11},{9,10},{10,... | collective-permute-start | bytes 3244040 | tf_op jit(solution)/shard_map/ppermute | solution.py:471

commit v2 on v1

v2 whole, which is shorter than its diff:
```python
import functools

import jax
import jax.numpy as jnp
import numpy as np
from jax import lax
from jax.experimental import pallas as pl
from jax.experimental.pallas import tpu as pltpu
from jax.sharding import PartitionSpec as P

MESH = pl.DeviceIdType.MESH
SIDES = (10, 14, 18)
EPS = 1e-05
F32 = jnp.float32
BF16 = jnp.bfloat16
CT = 256
EARLY = 2
PIECES = (("c", 1), ("d", 2), ("b", 2)) * 4
KEEP = np.float32(1.0) / np.float32(0.9)
GELU_C = np.float32(np.sqrt(2.0 / np.pi))
GELU_K = np.float32(0.044715)


def up(value, unit):
    return -(-value // unit) * unit


def dot(a, b):
    return lax.dot_general(a, b, (((1,), (0,)), ((), ())), preferred_element_type=F32)


def dot_nt(a, b):
    return lax.dot_general(a, b, (((1,), (1,)), ((), ())), preferred_element_type=F32)


def dot_tn(a, b):
    return lax.dot_general(a, b, (((0,), (0,)), ((), ())), preferred_element_type=F32)


def gelu_both(z):
    z2 = z * z
    t = jnp.tanh(z * (GELU_C + (GELU_C * GELU_K) * z2))
    a = 0.5 + 0.5 * t
    g = z * a
    slope = a + (g * (1.0 - t)) * (GELU_C + (3.0 * GELU_C * GELU_K) * z2)
    return g, slope


def fold(v):
    total = v[:, :128]
    for i in range(1, v.shape[1] // 128):
        total = total + v[:, i * 128 : (i + 1) * 128]
    return total


def col8(v):
    return jnp.sum(v.reshape(v.shape[0] // 8, 8, v.shape[1]), axis=0)


def pack_kernel(slot_count, groups, me_ref, order_ref, img_ref, cot_ref, *refs):
    outs, (xf, yf, stage) = refs[:-3], refs[-3:]
    me = me_ref[0]
    count = img_ref.shape[1]
    lanes = xf.shape[0]

    @pl.loop(0, slot_count, unroll=9)
    def _(r):
        at = pl.ds(pl.multiple_of(r * count, 8), count)
        for c in range(lanes):
            xf[c, at, :] = img_ref[r, :, c * 128 : (c + 1) * 128].astype(F32)
            yf[c, at, :] = cot_ref[r, :, c * 128 : (c + 1) * 128].astype(F32)

    for j in range(outs[0].shape[0]):
        for k in range(groups):
            dest = me ^ k
            which = order_ref[j * groups + (dest if j % 2 == 0 else groups - 1 - dest)]
            for c in range(lanes):
                cols = slice(c * 128, (c + 1) * 128)
                stage[0:slot_count, cols] = xf[c, pl.ds(which, slot_count, stride=count), :]
                stage[slot_count : 2 * slot_count, cols] = yf[c, pl.ds(which, slot_count, stride=count), :]
            outs[k][j] = stage[...].astype(BF16)


def unpack_kernel(slot_count, quarter, rank_ref, key_ref, img_ref, cot_ref, back_ref, out_ref, grad_ref, xf, yf, stage):
    lanes = xf.shape[0]
    count = img_ref.shape[1]

    @pl.loop(0, slot_count, unroll=9)
    def _(r):
        at = pl.ds(pl.multiple_of(r * count, 8), count)
        for c in range(lanes):
            xf[c, at, :] = img_ref[r, :, c * 128 : (c + 1) * 128].astype(F32)
            yf[c, at, :] = cot_ref[r, :, c * 128 : (c + 1) * 128].astype(F32)

    @pl.loop(0, count)
    def _(i):
        key = key_ref[i]
        for c, q in enumerate(quarter):

            @pl.when(key == c + 1)
            def _(q=q):
                stage[...] = back_ref[rank_ref[i]].astype(F32)
                at = pl.ds(i, q, stride=count)
                for b in range(lanes):
                    cols = slice(b * 128, (b + 1) * 128)
                    xf[b, at, :] = xf[b, at, :] + stage[0:q, cols]
                    yf[b, at, :] = yf[b, at, :] + stage[slot_count : slot_count + q, cols]

    @pl.loop(0, slot_count, unroll=9)
    def _(r):
        at = pl.ds(pl.multiple_of(r * count, 8), count)
        for c in range(lanes):
            out_ref[r, :, c * 128 : (c + 1) * 128] = xf[c, at, :].astype(BF16)
            grad_ref[r, :, c * 128 : (c + 1) * 128] = yf[c, at, :]


def widen_kernel(first, src_ref, in_ref, out_ref):
    t = pl.program_id(0)

    @pl.when(t < first)
    def _():
        in_ref[...] = src_ref[...].astype(F32)

    @pl.when(t >= first)
    def _():
        out_ref[...] = src_ref[...].astype(F32).T


def image_work(kind, slot, slot_count, me, parcel, par, acc, scr):
    groups = parcel.shape[0]
    rows = scr["xs"].shape[0]
    width = scr["xs"].shape[1]
    half = scr["gate"].shape[1]
    tiles = half // CT
    xs, dys, stage, act, dbr = scr["xs"], scr["dys"], scr["stage"], scr["act"], scr["dbr"]
    vs, gvp, gate, gated, dsp, dgs, dpre = (
        scr["vs"], scr["gvp"], scr["gate"], scr["gated"], scr["dsp"], scr["dgs"], scr["dpre"],
    )
    for m in range(groups):

        @pl.when(me == m)
        def _(m=m):
            for k in range(groups):
                at = (m ^ k) * slot_count
                stage[...] = parcel.at[k, slot][...].astype(F32)
                xs[at : at + slot_count, :] = stage[0:slot_count, :]
                dys[at : at + slot_count, :] = stage[slot_count : 2 * slot_count, :]

    x = xs[0:rows, :]
    mean = jnp.mean(x, axis=-1, keepdims=True)
    cen = x - mean
    inv = lax.rsqrt(jnp.mean(cen * cen, axis=-1, keepdims=True) + EPS)
    xhat = cen * inv
    xs[0:rows, :] = xhat
    scr["inv"][0:rows, :] = jnp.broadcast_to(inv, (rows, 128))
    act[0:rows, :] = (xhat * par["ln_gain"][...] + par["ln_bias"][...]).astype(BF16)
    db = (dys[0:rows, :] * par["live"][kind, :, 0:1]).astype(BF16)
    dbr[0:rows, :] = db
    acc["b_out"][...] += col8(db.astype(F32))

    @pl.loop(0, tiles, unroll=tiles)
    def _(t):
        at = pl.ds(pl.multiple_of(t * CT, CT), CT)
        far = pl.ds(pl.multiple_of(half + t * CT, CT), CT)
        z = dot(act[0:rows, :], par["w_in"][:, far]) + par["b_in"][:, far]
        g, slope = gelu_both(z)
        vs[0:rows, at] = g
        gvp[0:rows, at] = slope.astype(BF16)

    total = fold(vs[0:rows, :])
    vmean = jnp.sum(total, axis=-1, keepdims=True) / half
    cen = vs[0:rows, :] - vmean
    vinv = lax.rsqrt(jnp.sum(fold(cen * cen), axis=-1, keepdims=True) / half + EPS)
    vhat = cen * vinv
    vs[0:rows, :] = vhat
    gate[0:rows, :] = (vhat * par["gate_gain"][...] + par["gate_bias"][...]).astype(BF16)
    last = lax.broadcasted_iota(jnp.int32, (16, 1), 0) == 15
    gate[rows - 16 : rows, :] = jnp.where(last, 1.0, gate[rows - 16 : rows, :].astype(F32)).astype(BF16)
    scr["hs"][0:rows, :] = jnp.zeros((rows, 128), F32)
    scr["hv"][0:rows, :] = jnp.zeros((rows, 128), F32)

    @pl.loop(0, tiles, unroll=tiles)
    def _(t):
        at = pl.ds(pl.multiple_of(t * CT, CT), CT)
        z = dot(act[0:rows, :], par["w_in"][:, at]) + par["b_in"][:, at]
        u, slope = gelu_both(z)
        sp = dot(par["wsp"][kind], gate[0:rows, at]) + par["bsp"][kind, :, 0:1]
        gated[0:rows, at] = (u * sp).astype(BF16)
        dg = dot_nt(dbr[0:rows, :], par["w_out"][at, :])
        pre = (dg * sp * slope).astype(BF16)
        dpre[0:rows, at] = pre
        ds = (dg * u).astype(BF16)
        dsp[0:rows, at] = ds
        dgate = dot(par["wsp_t"][kind], ds)
        vh = vs[0:rows, at]
        acc["gate_bias"][:, at] += col8(dgate)
        acc["gate_gain"][:, at] += col8(dgate * vh)
        h = dgate * par["gate_gain"][:, at]
        dgs[0:rows, at] = h
        scr["hs"][0:rows, :] += fold(h)
        scr["hv"][0:rows, :] += fold(h * vh)

    hmean = jnp.sum(scr["hs"][0:rows, :], axis=-1, keepdims=True) / half
    hvmean = jnp.sum(scr["hv"][0:rows, :], axis=-1, keepdims=True) / half

    @pl.loop(0, tiles, unroll=tiles)
    def _(t):
        at = pl.ds(pl.multiple_of(t * CT, CT), CT)
        far = pl.ds(pl.multiple_of(half + t * CT, CT), CT)
        dv = vinv * (dgs[0:rows, at] - hmean - vs[0:rows, at] * hvmean)
        pre = (dv * gvp[0:rows, at].astype(F32)).astype(BF16)
        dpre[0:rows, far] = pre

    mixed = dot_nt(dsp[0:rows, :], gate[0:rows, :])
    for c in range(acc["w_sp"].shape[0]):
        acc["w_sp"][c, :, 0:rows] += jnp.where(kind == c + 1, mixed, 0.0)
    branch = dot(gated[0:rows, :], par["w_out"][...]) + par["b_out"][...]
    dys[0:rows, :] = branch * KEEP
    dact = dot_nt(dpre[0:rows, :], par["w_in"][...])
    xhat = xs[0:rows, :]
    acc["ln_bias"][...] += col8(dact)
    acc["ln_gain"][...] += col8(dact * xhat)
    h = dact * par["ln_gain"][...]
    back = scr["inv"][0:rows, 0:1] * (
        h - jnp.mean(h, axis=-1, keepdims=True) - xhat * jnp.mean(h * xhat, axis=-1, keepdims=True)
    )
    xs[0:rows, :] = back
    for m in range(groups):

        @pl.when(me == m)
        def _(m=m):
            for k in range(groups):
                at = (m ^ k) * slot_count
                stage[0:slot_count, :] = dys[at : at + slot_count, :]
                stage[slot_count : 2 * slot_count, :] = xs[at : at + slot_count, :]
                parcel[k, slot] = stage[...].astype(BF16)


PAR = ("ln_gain", "ln_bias", "w_in", "b_in", "gate_gain", "gate_bias", "wsp", "wsp_t", "bsp", "live", "pick", "w_out", "b_out")
ACC = ("w_sp", "gate_gain", "gate_bias", "ln_gain", "ln_bias", "b_out", "w_in", "w_out")
SCR = ("stage", "xs", "dys", "inv", "vs", "gvp", "gate", "dsp", "dgs", "hs", "hv")
KEPT = ("act", "dbr", "gated", "dpre")


def reduce_orders(dp):
    bits = [("dp", 1 << b) for b in range(dp.bit_length() - 1)]
    x, z, y = bits[:1], bits[1:], [("patch", 2)]
    return {"a": x + y + z, "b": y + x + z, "c": z + x + y, "d": x + z + y, "e": y + z + x, "f": z + y + x}

def plan_sizes(depth, rows):
    sizes = [rows]
    for _ in range(depth):
        sizes.append(sizes[-1] // 2 if sizes[-1] // 2 >= 16 else sizes[-1])
    return sizes

LINES = ("gate_gain", "gate_bias", "ln_gain", "ln_bias", "b_out")


def gather_gradients(total_ref, par, acc, kept):
    act_t = jnp.concatenate([kept["act"][...].T, jnp.ones((16, kept["act"].shape[0]), BF16)], axis=0)
    for t in range(acc["w_in"].shape[1] // CT):
        at = slice(t * CT, (t + 1) * CT)
        acc["w_in"][:, at] += dot(act_t, kept["dpre"][:, at])
    dbr_t = kept["dbr"][...].T
    for t in range(acc["w_out"].shape[1] // CT):
        at = slice(t * CT, (t + 1) * CT)
        acc["w_out"][:, at] += dot(dbr_t, kept["gated"][:, at])


def lay_out(total_ref, par, acc):
    width, half = acc["w_out"].shape
    wide = acc["w_in"].shape[1]
    base = wide + half
    rows, span = acc["w_sp"].shape[1:]
    total_ref[:, 0:wide] = acc["w_in"][0:width, :].astype(BF16)
    total_ref[:, wide:base] = acc["w_out"][...].astype(BF16)
    mix = acc["w_sp"][2, :, 0:rows]
    for c in range(2):
        pick = par["pick"][c]
        part = dot(acc["w_sp"][c, :, 0:rows].astype(BF16), pick).astype(BF16)
        mix = mix + dot(par["pick"][2 + c], part)
    total_ref[:, base:] = jnp.zeros((width, total_ref.shape[1] - base), BF16)
    total_ref[0:rows, base : base + rows] = mix.astype(BF16)
    lines = []
    for name in LINES:
        v = jnp.sum(acc[name][...], axis=0, keepdims=True)
        lines += [v[:, i * width : (i + 1) * width] for i in range(v.shape[1] // width)]
    lines.append(jnp.zeros((16 - len(lines), width), F32))
    more = [acc["w_in"][width : width + 1, i * width : (i + 1) * width] for i in range(wide // width)]
    more.append(jnp.zeros((16 - len(more), width), F32))
    total_ref[rows : rows + 32, base : base + width] = jnp.concatenate(lines + more, axis=0).astype(BF16)


def layer_kernel(orders, spans, sizes, slot_count, groups, pair, cls_ref, *refs):
    depth = len(orders[0])
    packed, refs = refs[:groups], refs[groups:]
    par, refs = dict(zip(PAR, refs)), refs[len(PAR) :]
    out_ref, back_ref, total_ref, parcel, *refs = refs
    acc, refs = dict(zip(ACC, refs)), refs[len(ACC) :]
    scr, refs = dict(zip(SCR, refs)), refs[len(SCR) :]
    kept, refs = dict(zip(KEPT, refs)), refs[len(KEPT) :]
    first, *refs = refs
    rbufs, refs = refs[:depth], refs[depth:]
    send_sem, recv_sem, in_send, in_recv, back_send, back_recv, own_sem = refs
    dp, patch = lax.axis_index("dp"), lax.axis_index("patch")
    core = patch & 1

    def peer(axis, bit):
        return (dp ^ bit, patch) if axis == "dp" else (dp, patch ^ bit)

    peers = [peer("patch", 1), peer("patch", 3)] + [peer(a, b) for a, b in orders[0]]
    barrier = pltpu.get_barrier_semaphore()
    for other in peers:
        pl.semaphore_signal(barrier, inc=1, device_id=other, device_id_type=MESH)
    pl.semaphore_wait(barrier, len(peers))

    slots = parcel.shape[1]

    def inward(k, j):
        if k == 0:
            return pltpu.make_async_copy(packed[0].at[j], parcel.at[0, j], own_sem.at[0, j])
        return pltpu.make_async_remote_copy(
            src_ref=packed[k].at[j], dst_ref=parcel.at[k, j], send_sem=in_send.at[k, j], recv_sem=in_recv.at[k, j],
            device_id=peer("patch", k), device_id_type=MESH,
        )

    def back(k, j):
        place = j * groups + jnp.where(lax.rem(j, 2) == 0, patch, groups - 1 - patch)
        if k == 0:
            return pltpu.make_async_copy(parcel.at[0, j], back_ref.at[place], own_sem.at[1, j])
        return pltpu.make_async_remote_copy(
            src_ref=parcel.at[k, j], dst_ref=back_ref.at[place], send_sem=back_send.at[k, j], recv_sem=back_recv.at[k, j],
            device_id=peer("patch", k), device_id_type=MESH,
        )

    @pl.loop(0, slots)
    def _(j):
        for k in range(groups - 1, -1, -1):
            inward(k, j).start()

    for ref in acc.values():
        ref[...] = jnp.zeros_like(ref)
    rows = scr["xs"].shape[0]
    for ref in kept.values():
        if ref.shape[0] > pair * rows:
            ref[pair * rows :, :] = jnp.zeros((ref.shape[0] - pair * rows, ref.shape[1]), BF16)
    n = groups * slot_count
    for name in ("xs", "dys"):
        scr[name][rows - 16 : rows, :] = jnp.zeros((16, scr[name].shape[1]), F32)

    @pl.loop(0, slots)
    def _(j):
        for k in range(groups):
            inward(k, j).wait()
        half_at = pl.ds(pl.multiple_of(lax.rem(j, pair) * rows, 16), rows)
        views = {name: ref.at[half_at] for name, ref in kept.items()}
        image_work(cls_ref[j], j, slot_count, patch, parcel, par, acc, scr | views)

        @pl.when(lax.rem(j, pair) == pair - 1)
        def _():
            gather_gradients(total_ref, par, acc, kept)

    lay_out(total_ref, par, acc)
    half = total_ref.shape[1] // 2
    tall = total_ref.shape[0]
    pieces = len(orders)
    mine = pl.multiple_of(core * half, 128)
    theirs = pl.multiple_of((1 - core) * half, 128)
    copies = []

    def send(src, dst, step, i, other):
        copy = pltpu.make_async_remote_copy(
            src_ref=src, dst_ref=dst, send_sem=send_sem.at[step, i], recv_sem=recv_sem.at[step, i], device_id=other,
            device_id_type=MESH,
        )
        copy.start()
        copies.append(copy)
        return copy

    def cols(i):
        return pl.ds(spans[i][0], spans[i][1])

    def shifted(base, i):
        return pl.ds(pl.multiple_of(base + spans[i][0], 128), spans[i][1])

    def high(axis, bit):
        return jnp.where(((dp if axis == "dp" else patch) & bit) != 0, 1, 0)

    def give_back(begin, end):
        @pl.loop(begin, end)
        def _(j):
            for k in range(groups - 1, -1, -1):
                back(k, j).start()

    state = [0] * pieces
    flying = [
        send(total_ref.at[:, shifted(theirs, i)], first.at[:, cols(i)], 0, i, peer("patch", 1)) for i in range(pieces)
    ]
    early = slots * EARLY // 6
    give_back(0, early)
    for s in range(depth + 1):
        for i in range(pieces):
            flying[i].wait_recv()
            lo = state[i]
            if s > 0 and sizes[s - 1] == sizes[s]:
                flying[i].wait_send()
                copies[:] = [copy for copy in copies if copy is not flying[i]]
            got_ref = first if s == 0 else rbufs[s - 1]
            unit = 32 if sizes[s] % 32 == 0 else 16

            @pl.loop(0, sizes[s], step=unit)
            def _(r, i=i, lo=lo, got_ref=got_ref, unit=unit):
                at = pl.ds(pl.multiple_of(lo + r, 16), unit)
                got = pl.ds(pl.multiple_of(r, 16), unit)
                total_ref[at, shifted(mine, i)] = (
                    total_ref[at, shifted(mine, i)].astype(F32) + got_ref[got, cols(i)].astype(F32)
                ).astype(BF16)

            if s < depth:
                axis, bit = orders[i][s]
                keep = sizes[s + 1]
                give = state[i]
                if keep < sizes[s]:
                    give = pl.multiple_of(state[i] + (1 - high(axis, bit)) * keep, 16)
                    state[i] = pl.multiple_of(state[i] + high(axis, bit) * keep, 16)
                flying[i] = send(
                    total_ref.at[pl.ds(give, keep), shifted(mine, i)], rbufs[s].at[pl.ds(0, keep), cols(i)], s + 1, i,
                    peer(axis, bit),
                )
    for i in range(pieces):
        at = pl.ds(pl.multiple_of(state[i], 16), sizes[depth])
        out_ref[at, shifted(mine, i)] = total_ref[at, shifted(mine, i)]
    flying = [None] * pieces
    for s in range(depth, -1, -1):
        if s == depth - 2:
            give_back(early, slots)
        for i in range(pieces):
            if flying[i] is not None:
                flying[i].wait_recv()
                flying[i] = None
            step = 2 * depth + 1 - s
            if s == 0:
                where = out_ref.at[:, shifted(mine, i)]
                flying[i] = send(where, where, step, i, peer("patch", 1))
            elif sizes[s] < sizes[s - 1]:
                axis, bit = orders[i][s - 1]
                where = out_ref.at[pl.ds(pl.multiple_of(state[i], 16), sizes[s]), shifted(mine, i)]
                flying[i] = send(where, where, step, i, peer(axis, bit))
                state[i] = state[i] - high(axis, bit) * sizes[s]
    for i in range(pieces):
        flying[i].wait_recv()

    @pl.loop(0, slots)
    def _(j):
        for k in range(groups):
            back(k, j).wait()

    for copy in copies:
        copy.wait_send()


def call_layer(cls, packed, par, dp, groups, slot_count, pieces):
    slots, stage_rows, width = packed[0].shape
    wide, half, side = par["w_in"].shape[1], par["w_out"].shape[0], par["wsp"].shape[1]
    span = up(side, 128)
    pair = 2 if slots % 2 == 0 else 1
    columns = wide + half + width
    table = reduce_orders(dp)
    orders = [table[name] for name, _ in pieces]
    starts = np.cumsum([0] + [w * 128 for _, w in pieces])
    spans = [(int(starts[i]), w * 128) for i, (_, w) in enumerate(pieces)]
    depth = len(orders[0])
    sizes = plan_sizes(depth, width)
    vmem = pl.BlockSpec(memory_space=pltpu.VMEM)
    far = pl.BlockSpec(memory_space=pl.ANY)
    acc = {
        "w_sp": (3, side, span), "gate_gain": (8, half), "gate_bias": (8, half), "ln_gain": (8, width),
        "ln_bias": (8, width), "b_out": (8, width), "w_in": (width + 16, wide), "w_out": (width, half),
    }
    scr = {
        "stage": ((stage_rows, width), F32), "xs": ((side, width), F32), "dys": ((side, width), F32),
        "inv": ((side, 128), F32), "vs": ((side, half), F32), "gvp": ((side, half), BF16), "gate": ((side, half), BF16),
        "dsp": ((side, half), BF16), "dgs": ((side, half), F32), "hs": ((side, 128), F32), "hv": ((side, 128), F32),
    }
    room = up(pair * side, 256)
    return pl.pallas_call(
        functools.partial(layer_kernel, orders, spans, sizes, slot_count, groups, pair),
        out_shape=[
            jax.ShapeDtypeStruct((width, columns), BF16),
            jax.ShapeDtypeStruct((slots * groups, stage_rows, width), BF16),
        ],
        in_specs=[pl.BlockSpec(memory_space=pltpu.SMEM)] + [far] * groups + [vmem] * len(PAR),
        out_specs=[vmem, far],
        scratch_shapes=[pltpu.VMEM((width, columns), BF16), pltpu.VMEM((groups, slots, stage_rows, width), BF16)]
        + [pltpu.VMEM(acc[name], F32) for name in ACC]
        + [pltpu.VMEM(*scr[name]) for name in SCR]
        + [pltpu.VMEM((room, n), BF16) for n in (width, width, half, wide)]
        + [pltpu.VMEM((width, columns // 2), BF16)]
        + [pltpu.VMEM((size, columns // 2), BF16) for size in sizes[1:]]
        + [pltpu.SemaphoreType.DMA((2 * depth + 2, len(pieces)))] * 2
        + [pltpu.SemaphoreType.DMA((groups, slots))] * 4
        + [pltpu.SemaphoreType.DMA((2, slots))],
        compiler_params=pltpu.CompilerParams(
            collective_id=1, has_side_effects=True, vmem_limit_bytes=64 * 1024 * 1024 - 65536
        ),
        name="layer",
    )(cls, *packed, *[par[name] for name in PAR])


def local(images, cotangent, res_class, skip, ln_gain, ln_bias, w_in, b_in, gate_gain, gate_bias, w_spatial, b_spatial, w_out, b_out):
    groups = lax.axis_size("patch")
    dp = lax.axis_size("dp")
    count, slot_count, width = images.shape
    half = w_out.shape[0]
    wide = w_in.shape[1]
    slots = count // groups
    quarter = tuple(side * side // groups for side in SIDES)
    patches = groups * slot_count
    side = up(patches, 16)
    span = up(patches, 128)
    stage_rows = up(2 * slot_count, 16)
    me = lax.axis_index("patch").astype(jnp.int32)

    key = jnp.where(skip != 0, res_class + 1, 0).astype(jnp.int32)
    index = jnp.arange(count, dtype=jnp.int32)
    before = (key[None, :] > key[:, None]) | ((key[None, :] == key[:, None]) & (index[None, :] < index[:, None]))
    rank = jnp.sum(before.astype(jnp.int32), axis=1)
    hit = rank[None, :] == index[:, None]
    order = jnp.sum(jnp.where(hit, index[None, :], 0), axis=1)
    slot_index = jnp.arange(slots, dtype=jnp.int32)
    spot = slot_index * groups + jnp.where(slot_index % 2 == 0, me, groups - 1 - me)
    cls = jnp.sum(jnp.where(spot[:, None] == rank[None, :], key[None, :], 0), axis=1)
    me1 = me.reshape(1)

    whole = pl.BlockSpec(memory_space=pltpu.VMEM)
    smem = pl.BlockSpec(memory_space=pltpu.SMEM)
    img_t = jnp.swapaxes(images, 0, 1)
    cot_t = jnp.swapaxes(cotangent, 0, 1)
    planes = (width // 128, slot_count * count, 128)
    packed = pl.pallas_call(
        functools.partial(pack_kernel, slot_count, groups),
        out_shape=[jax.ShapeDtypeStruct((slots, stage_rows, width), BF16)] * groups,
        in_specs=[smem, smem, whole, whole],
        out_specs=[whole] * groups,
        scratch_shapes=[pltpu.VMEM(planes, F32), pltpu.VMEM(planes, F32), pltpu.VMEM((stage_rows, width), F32)],
        compiler_params=pltpu.CompilerParams(vmem_limit_bytes=40 * 1024 * 1024),
        name="pack",
    )(me1, order, img_t, cot_t)

    live, where = [], []
    at = jnp.arange(side, dtype=jnp.int32)
    place, within = at // slot_count, at % slot_count
    for q in quarter:
        live.append((within < q) & (at < patches))
        where.append(jnp.where(live[-1], place * q + within, -1))
    picks = [(w[:, None] == at[None, :]).astype(BF16) for w in where]
    w_pad = jnp.pad(w_spatial, ((0, side - patches),) * 2)
    b_pad = jnp.pad(b_spatial, (0, side - patches))
    spread = [jnp.zeros((side, side), BF16)]
    bias = [jnp.zeros((side,), F32)]
    for c, pick in enumerate(picks):
        if c < 2:
            moved = jnp.einsum("ta,ab->tb", pick, w_pad, preferred_element_type=F32).astype(BF16)
            spread.append(jnp.einsum("tb,sb->ts", moved, pick, preferred_element_type=F32).astype(BF16))
            bias.append(jnp.sum(jnp.where(where[c][:, None] == at[None, :], b_pad[None, :], 0.0), axis=1))
        else:
            spread.append(w_pad)
            bias.append(b_pad)
    wsp = jnp.stack(spread)
    wsp_t = jnp.swapaxes(wsp, 1, 2)
    bsp = jnp.stack([jnp.broadcast_to(v[:, None], (side, 128)) for v in bias])
    keep = jnp.stack([jnp.zeros((side, 128), F32)] + [jnp.broadcast_to(jnp.where(v, KEEP, 0.0)[:, None], (side, 128)) for v in live])
    corner = ((at[:, None] == side - 1) & (at[None, :] == side - 1)).astype(BF16)
    lift = [pick + corner for pick in picks[:2]]
    pick = jnp.stack(lift + [v.T for v in lift])
    par = {
        "ln_gain": ln_gain[None, :], "ln_bias": ln_bias[None, :], "w_in": w_in, "b_in": b_in[None, :],
        "gate_gain": gate_gain[None, :], "gate_bias": gate_bias[None, :], "wsp": wsp, "wsp_t": wsp_t, "bsp": bsp, "live": keep, "pick": pick,
        "w_out": w_out, "b_out": b_out[None, :],
    }
    summed, backs = call_layer(cls, packed, par, dp, groups, slot_count, PIECES)
    out_t, grad_t = pl.pallas_call(
        functools.partial(unpack_kernel, slot_count, quarter),
        out_shape=[jax.ShapeDtypeStruct((slot_count, count, width), BF16), jax.ShapeDtypeStruct((slot_count, count, width), F32)],
        in_specs=[smem, smem] + [whole] * 3,
        out_specs=[whole, whole],
        scratch_shapes=[pltpu.VMEM(planes, F32), pltpu.VMEM(planes, F32), pltpu.VMEM((stage_rows, width), F32)],
        compiler_params=pltpu.CompilerParams(vmem_limit_bytes=40 * 1024 * 1024),
        name="unpack",
    )(rank, key, img_t, cot_t, backs)
    output = jnp.swapaxes(out_t, 0, 1)
    grad_images = jnp.swapaxes(grad_t, 0, 1)

    cut = 2 * CT
    first, last = wide // cut, (wide + half) // cut
    g_w_in, g_w_out = pl.pallas_call(
        functools.partial(widen_kernel, first),
        out_shape=[jax.ShapeDtypeStruct((width, wide), F32), jax.ShapeDtypeStruct((half, width), F32)],
        grid=(last,),
        in_specs=[pl.BlockSpec((width, cut), lambda t: (0, t))],
        out_specs=[
            pl.BlockSpec((width, cut), lambda t: (0, jnp.minimum(t, first - 1))),
            pl.BlockSpec((cut, width), lambda t: (jnp.maximum(t - first, 0), 0)),
        ],
        name="widen",
    )(summed)
    base = wide + half
    small = summed[0 : side + 32, base:].astype(F32)
    lines = small[side : side + 16].reshape(-1)
    ends = np.cumsum([0, half, half, width, width, width])
    g_gate_gain, g_gate_bias, g_ln_gain, g_ln_bias, g_b_out = [lines[ends[i] : ends[i + 1]] for i in range(5)]
    g_b_in = small[side + 16 : side + 32].reshape(-1)[:wide]
    return (
        output, grad_images, g_ln_gain, g_ln_bias, g_w_in, g_b_in, g_gate_gain, g_gate_bias,
        small[:patches, :patches], small[:patches, side - 1], g_w_out, g_b_out,
    )


def solution(mesh):
    placed = (P("dp", "patch", None),) * 2 + (P("dp"),) * 2 + (P(),) * 10
    return jax.shard_map(
        local, mesh=mesh, in_specs=placed, out_specs=(P("dp", "patch", None),) * 2 + (P(),) * 10, check_vma=False,
    )
```

time: 320 us -> 222 us (0.69)
  waiting for transfers between devices: 69.2 us -> 0 us
  local copies, waits for them, and re-layouts: 36.8 us -> 20.2 us
  starting transfers between devices: 4.94 us -> 0 us
  Pallas kernels: 195 us -> 191 us
    ppermute x6 -> x0, waiting for transfers between devices: 69.2 us -> none  [swap(): lax.ppermute(parts[k], 'patch', [(i, i ^ k) for i in range(groups)])]
    unnamed x30 -> x29, local copies, waits for them, and re-layouts: 28 us -> 10.8 us
    ppermute x6 -> x0, starting transfers between devices: 4.94 us -> none  [swap(): lax.ppermute(parts[k], 'patch', [(i, i ^ k) for i in range(groups)])]
    convert_element_type x3 -> x1, other arithmetic: 5.85 us -> 1.21 us  [local(): small = summed[0:side + 32, base:].astype(F32)]
  transfers between devices with their start and end apart: 6 -> 0, of which waited for: 4 -> 0; matrix products, arithmetic and copies ran while one was open for 8% -> 0% of each run, Pallas kernels for 0% -> 0%
where the time goes in v2:
time: 222 us
  Pallas kernels  191 us (86%)
  local copies, waits for them, and re-layouts  20.2 us (9%)
  other arithmetic  8.6 us (4%)
    pallas_call x1, Pallas kernels, call_layer(): pl.pallas_call(functools.partial(layer_kernel, orders, spans, sizes, slot...  172 us
    unnamed x29, local copies, waits for them, and re-layouts  10.8 us
    pallas_call x1, Pallas kernels, local(): pl.pallas_call(functools.partial(widen_kernel, first), out_shape=[jax.Sha...  8.97 us
    pallas_call x1, Pallas kernels, local(): pl.pallas_call(functools.partial(unpack_kernel, slot_count, quarter), out...  6.54 us

profile of v2, /device:TPU:1, one launch (start us, length us, event | category | flops | bytes accessed | tf_op | source)
XLA Modules:
  0.0 221.6 jit_solution(10152676806232234352)
XLA Ops:
  0.7 0.7 compare_select_fusion.1.key_ref
  1.5 0.4 copy-done.9
  1.9 0.7 select_reduce_fusion.3.cls_ref
  2.7 0.7 pad.9
  3.8 1.3 broadcast_in_dim.119.refs_8_
  5.1 1.3 broadcast_in_dim.120.refs_9_
  7.0 1.1 copy.34
  8.2 0.7 fusion.1
  8.9 0.7 fusion
  9.6 1.3 pad_maximum_fusion.3
  11.3 1.2 pad_maximum_fusion.1.refs_14_
  12.5 1.2 fusion.38.refs_11_
  13.7 1.3 pad_maximum_fusion
  15.0 1.4 copy.37.refs_10_
  16.4 1.6 copy-done.2
  18.0 3.4 %pack.1 = (bf16[6,176,512]{2,1,0:T(8,128)(2,1)S(1)}, bf16[6,176,512]{2,1,0:T(8,128)(2,1)S(1)}, bf16[6,176,512]{2,1,0:T(8,128)(2,1)S(1)}, bf16[6,176,512]{2,1,0:T(8,128)(2,1)S(1)}) custom-call(s32[1]{0:T(128)} %bitcast.2.me_ref, s32[24]{0:T(128)S(1)} %select_reduce_fusion.2.order_ref, bf16[81,24,512]{2,1,0:T(8,128)(2,1)S(1)} %bitcast.22, ...), custom_call_target="tpu_custom_call" | custom-call | tf_op jit(solution)/shard_map/pack/pallas_call | solution.py:540
  21.4 1.0 copy-done.5
  22.3 1.0 copy-done.6
  23.3 1.0 copy-done.7
  24.3 1.0 copy-done.8
  25.3 171.8 %layer.1 = (bf16[512,5120]{1,0:T(8,128)(2,1)}, bf16[24,176,512]{2,1,0:T(8,128)(2,1)}) custom-call(s32[6]{0:T(128)} %select_reduce_fusion.3.cls_ref, bf16[6,176,512]{2,1,0:T(8,128)(2,1)} %copy-done.5, bf16[6,176,512]{2,1,0:T(8,128)(2,1)} %copy-done.6, bf16[6,176,512]{2,1,0:T(8,128)(2,1)} %copy-done.7, bf16[6,176,512]{2,1,0:T(8,128)(2,1)} %copy-done.8, ...), custom_call_target="tpu_custom_call" | custom-call | tf_op jit(solution)/shard_map/layer/pallas_call | solution.py:486
  197.1 1.2 slice_convert_fusion
  198.3 0.8 slice_reduce_fusion
  199.1 0.6 fusion.36
  199.7 0.6 slice.59
  200.3 0.8 slice.73
  201.1 0.6 slice.63
  201.7 0.6 slice.61
  202.4 1.5 copy-done.3
  203.9 2.2 %copy-done.4 = bf16[24,176,512]{2,1,0:T(8,128)(2,1)S(1)} copy-done((bf16[24,176,512]{2,1,0:T(8,128)(2,1)S(1)}, bf16[24,176,512]{2,1,0:T(8,128)(2,1)}, u32[]{:S(2)}) %copy-start.4) | copy-done | bytes 4325400
  206.1 6.5 %unpack.1 = (bf16[81,24,512]{2,1,0:T(8,128)(2,1)}, f32[81,24,512]{2,1,0:T(8,128)}) custom-call(s32[24]{0:T(128)S(1)} %copy-done.12, s32[24]{0:T(128)S(1)} %copy-done.10, bf16[81,24,512]{2,1,0:T(8,128)(2,1)S(1)} %bitcast.23, bf16[81,24,512]{2,1,0:T(8,128)(2,1)S(1)} %bitcast.25, bf16[24,176,512]{2,1,0:T(8,128)(2,1)S(1)} %copy-done.4), custom_call_target="tpu_custom_call" | custom-call | tf_op jit(solution)/shard_map/unpack/pallas_call | solution.py:582
  212.7 9.0 %widen.1 = (f32[512,3072]{1,0:T(8,128)}, f32[1536,512]{1,0:T(8,128)}) custom-call(bf16[512,5120]{1,0:T(8,128)(2,1)} %get-tuple-element.29.src_ref), custom_call_target="tpu_custom_call" | custom-call | tf_op jit(solution)/shard_map/widen/pallas_call | solution.py:596
  (41 shorter events, 1.7 us)
Async XLA Ops:
  1.3 0.6 copy-start.9
  1.9 0.7 copy-start.11
  9.6 2.9 %copy-start.13 = (bf16[1,336,336]{1,2,0:T(8,128)(2,1)}, bf16[1,336,336]{1,2,0:T(8,128)(2,1)S(1)}, u32[]{:S(2)}) copy-start(bf16[1,336,336]{1,2,0:T(8,128)(2,1)S(1)} %fusion) | copy-start | bytes 677380
  13.7 2.7 %copy-start = (bf16[24,81,512]{2,0,1:T(8,128)(2,1)S(1)}, bf16[24,81,512]{2,0,1:T(8,128)(2,1)}, u32[]{:S(2)}) copy-start(bf16[24,81,512]{2,0,1:T(8,128)(2,1)} %param.14) | copy-start | bytes 5971972
  16.4 1.6 copy-start.2
  21.3 1.0 copy-start.5
  22.3 1.0 copy-start.6
  23.3 1.0 copy-start.7
  24.3 1.0 copy-start.8
  197.1 5.3 %copy-start.1 = (bf16[24,81,512]{2,0,1:T(8,128)(2,1)S(1)}, bf16[24,81,512]{2,0,1:T(8,128)(2,1)}, u32[]{:S(2)}) copy-start(bf16[24,81,512]{2,0,1:T(8,128)(2,1)} %param.14) | copy-start | bytes 5971972
  197.1 5.3 %copy-start.10 = (s32[24]{0:T(128)S(1)}, s32[24]{0:T(128)}, u32[]{:S(2)}) copy-start(s32[24]{0:T(128)} %copy-done.9) | copy-start | bytes 292
  197.1 5.3 %copy-start.12 = (s32[24]{0:T(128)S(1)}, s32[24]{0:T(128)}, u32[]{:S(2)}) copy-start(s32[24]{0:T(128)} %copy-done.11) | copy-start | bytes 292
  202.4 1.6 copy-start.3
  203.9 2.2 %copy-start.4 = (bf16[24,176,512]{2,1,0:T(8,128)(2,1)S(1)}, bf16[24,176,512]{2,1,0:T(8,128)(2,1)}, u32[]{:S(2)}) copy-start(bf16[24,176,512]{2,1,0:T(8,128)(2,1)} %get-tuple-element.26.back_ref) | copy-start | bytes 12976132

commit v3 on v2

--- a/solution.py
+++ b/solution.py
@@ -14,7 +14,7 @@
 F32 = jnp.float32
 BF16 = jnp.bfloat16
 CT = 256
-EARLY = 2
+BACKS = (4, 4, 4, 5)
 PIECES = (("c", 1), ("d", 2), ("b", 2)) * 4
 KEEP = np.float32(1.0) / np.float32(0.9)
 GELU_C = np.float32(np.sqrt(2.0 / np.pi))
@@ -58,7 +58,7 @@
 
 
 def pack_kernel(slot_count, groups, me_ref, order_ref, img_ref, cot_ref, *refs):
-    outs, (xf, yf, stage) = refs[:-3], refs[-3:]
+    outs, (hold, xf, yf, stage, sem) = refs[:-5], refs[-5:]
     me = me_ref[0]
     count = img_ref.shape[1]
     lanes = xf.shape[0]
@@ -70,29 +70,77 @@
             xf[c, at, :] = img_ref[r, :, c * 128 : (c + 1) * 128].astype(F32)
             yf[c, at, :] = cot_ref[r, :, c * 128 : (c + 1) * 128].astype(F32)
 
-    for j in range(outs[0].shape[0]):
+    @pl.loop(0, outs[0].shape[0])
+    def _(j):
         for k in range(groups):
             dest = me ^ k
-            which = order_ref[j * groups + (dest if j % 2 == 0 else groups - 1 - dest)]
+            which = order_ref[j * groups + jnp.where(lax.rem(j, 2) == 0, dest, groups - 1 - dest)]
             for c in range(lanes):
                 cols = slice(c * 128, (c + 1) * 128)
                 stage[0:slot_count, cols] = xf[c, pl.ds(which, slot_count, stride=count), :]
                 stage[slot_count : 2 * slot_count, cols] = yf[c, pl.ds(which, slot_count, stride=count), :]
-            outs[k][j] = stage[...].astype(BF16)
-
-
-def unpack_kernel(slot_count, quarter, rank_ref, key_ref, img_ref, cot_ref, back_ref, out_ref, grad_ref, xf, yf, stage):
+            hold[k, j] = stage[...].astype(BF16)
+            pltpu.make_async_copy(hold.at[k, j], outs[k].at[j], sem.at[k, j]).start()
+
+    @pl.loop(0, outs[0].shape[0])
+    def _(j):
+        for k in range(groups):
+            pltpu.make_async_copy(hold.at[k, j], outs[k].at[j], sem.at[k, j]).wait()
+
+
+def finish_kernel(slot_count, quarter, wide, half, rank_ref, key_ref, img_far, cot_far, back_far, src_ref, *refs):
+    in_ref, out_w_ref, w_sp_ref, b_sp_ref, *refs = refs
+    lines, (out_ref, grad_ref, xf, yf, stage, out, grad, img_ref, cot_ref, back_ref, sem) = refs[:-11], refs[-11:]
     lanes = xf.shape[0]
     count = img_ref.shape[1]
-
-    @pl.loop(0, slot_count, unroll=9)
-    def _(r):
-        at = pl.ds(pl.multiple_of(r * count, 8), count)
-        for c in range(lanes):
-            xf[c, at, :] = img_ref[r, :, c * 128 : (c + 1) * 128].astype(F32)
-            yf[c, at, :] = cot_ref[r, :, c * 128 : (c + 1) * 128].astype(F32)
-
-    @pl.loop(0, count)
+    width, cut = src_ref.shape
+    t = pl.program_id(0)
+    small, first = 0, 1
+    last = first + (wide + half) // cut
+    part = -(-count // (last - 4))
+    copies = [pltpu.make_async_copy(out, out_ref, sem.at[0]), pltpu.make_async_copy(grad, grad_ref, sem.at[1])]
+    loads = [
+        pltpu.make_async_copy(a, b, sem.at[2 + i])
+        for i, (a, b) in enumerate(((img_far, img_ref), (cot_far, cot_ref), (back_far, back_ref)))
+    ]
+
+    @pl.when(t == small)
+    def _():
+        for load in loads:
+            load.start()
+        block = src_ref[...].astype(F32)
+        patches = w_sp_ref.shape[0]
+        side = up(patches, 16)
+        w_sp_ref[...] = block[:patches, :patches]
+        low = (side - 1) // 128 * 128
+        b_sp_ref[...] = block[:side, low : low + 128].T[side - 1 - low, :patches]
+        at = side
+        for ref in lines:
+            for n in range(ref.shape[0] // width):
+                ref[n * width : (n + 1) * width] = block[at, :]
+                at += 1
+
+    @pl.when(t == first)
+    def _():
+        for load in loads:
+            load.wait()
+
+        @pl.loop(0, slot_count, unroll=9)
+        def _(r):
+            at = pl.ds(pl.multiple_of(r * count, 8), count)
+            for c in range(lanes):
+                xf[c, at, :] = img_ref[r, :, c * 128 : (c + 1) * 128].astype(F32)
+                yf[c, at, :] = cot_ref[r, :, c * 128 : (c + 1) * 128].astype(F32)
+
+    @pl.when((t >= first) & (t < first + wide // cut))
+    def _():
+        in_ref[...] = src_ref[...].astype(F32)
+
+    @pl.when(t >= first + wide // cut)
+    def _():
+        out_w_ref[...] = src_ref[...].astype(F32).T
+
+    @pl.loop(jnp.clip((t - 2) * part, 0, count), jnp.clip((t - 1) * part, 0, count))
     def _(i):
         key = key_ref[i]
         for c, q in enumerate(quarter):
@@ -106,24 +154,22 @@
                     xf[b, at, :] = xf[b, at, :] + stage[0:q, cols]
                     yf[b, at, :] = yf[b, at, :] + stage[slot_count : slot_count + q, cols]
 
-    @pl.loop(0, slot_count, unroll=9)
-    def _(r):
-        at = pl.ds(pl.multiple_of(r * count, 8), count)
-        for c in range(lanes):
-            out_ref[r, :, c * 128 : (c + 1) * 128] = xf[c, at, :].astype(BF16)
-            grad_ref[r, :, c * 128 : (c + 1) * 128] = yf[c, at, :]
-
-
-def widen_kernel(first, src_ref, in_ref, out_ref):
-    t = pl.program_id(0)
-
-    @pl.when(t < first)
+    @pl.when(t == last - 2)
     def _():
-        in_ref[...] = src_ref[...].astype(F32)
-
-    @pl.when(t >= first)
+        @pl.loop(0, slot_count, unroll=9)
+        def _(r):
+            at = pl.ds(pl.multiple_of(r * count, 8), count)
+            for c in range(lanes):
+                out[r, :, c * 128 : (c + 1) * 128] = xf[c, at, :].astype(BF16)
+                grad[r, :, c * 128 : (c + 1) * 128] = yf[c, at, :]
+
+        for copy in copies:
+            copy.start()
+
+    @pl.when(t == last - 1)
     def _():
-        out_ref[...] = src_ref[...].astype(F32).T
+        for copy in copies:
+            copy.wait()
 
 
 def image_work(kind, slot, slot_count, me, parcel, par, acc, scr):
@@ -236,24 +282,63 @@
                 parcel[k, slot] = stage[...].astype(BF16)
 
 
-PAR = ("ln_gain", "ln_bias", "w_in", "b_in", "gate_gain", "gate_bias", "wsp", "wsp_t", "bsp", "live", "pick", "w_out", "b_out")
+VECTORS = ("b_in", "gate_gain", "gate_bias", "ln_gain", "ln_bias", "b_out", "b_sp")
+LARGE = ("w_in", "w_out")
+TABLES = ("wsp", "wsp_t", "bsp", "live", "pick")
 ACC = ("w_sp", "gate_gain", "gate_bias", "ln_gain", "ln_bias", "b_out", "w_in", "w_out")
 SCR = ("stage", "xs", "dys", "inv", "vs", "gvp", "gate", "dsp", "dgs", "hs", "hv")
 KEPT = ("act", "dbr", "gated", "dpre")
 
 
 def reduce_orders(dp):
-    bits = [("dp", 1 << b) for b in range(dp.bit_length() - 1)]
-    x, z, y = bits[:1], bits[1:], [("patch", 2)]
-    return {"a": x + y + z, "b": y + x + z, "c": z + x + y, "d": x + z + y, "e": y + z + x, "f": z + y + x}
-
-def plan_sizes(depth, rows):
+    bits = [1 << b for b in range(dp.bit_length() - 1)]
+    x, z, y = [("dp", bits[:1])], [("dp", [bit]) for bit in bits[1:3]], [("patch", [2])]
+    rest = [("dp", [bit]) for bit in bits[3:]]
+    return {
+        "a": x + y + z + rest, "b": y + x + z + rest, "c": z + x + y + rest, "d": x + z + y + rest, "e": y + z + x + rest,
+    }
+
+
+def combos(bits):
+    masks = [0]
+    for bit in bits:
+        masks += [mask | bit for mask in masks]
+    return masks[1:]
+
+
+def plan_sizes(order, rows):
     sizes = [rows]
-    for _ in range(depth):
-        sizes.append(sizes[-1] // 2 if sizes[-1] // 2 >= 16 else sizes[-1])
+    for _, bits in order:
+        keep = sizes[-1] >> len(bits)
+        sizes.append(keep if keep >= 16 else sizes[-1])
     return sizes
 
+
 LINES = ("gate_gain", "gate_bias", "ln_gain", "ln_bias", "b_out")
+
+
+def fill_tables(par, quarter, slot_count, groups):
+    side = par["w_sp"].shape[0]
+    t = lax.broadcasted_iota(jnp.int32, (side, 1), 0)
+    lane = lax.broadcasted_iota(jnp.int32, (1, side), 1)
+    place = sum(jnp.where(t >= slot_count * g, 1, 0) for g in range(1, groups))
+    within = t - slot_count * place
+    w = par["w_sp"][...]
+    for name in ("wsp", "wsp_t", "bsp", "live"):
+        par[name][0] = jnp.zeros(par[name].shape[1:], par[name].dtype)
+    for c, q in enumerate(quarter):
+        live = (within < q) & (t < slot_count * groups)
+        hit = live & (place * q + within == lane)
+        pick = jnp.where(hit, 1.0, 0.0)
+        low = pick.astype(BF16)
+        par["wsp"][c + 1] = dot_nt(dot(low, w).astype(BF16), low).astype(BF16)
+        par["wsp_t"][c + 1] = dot_nt(dot_nt(low, w).astype(BF16), low).astype(BF16)
+        bias = jnp.sum(jnp.where(hit, par["b_sp"][...], 0.0), axis=-1, keepdims=True)
+        par["bsp"][c + 1] = jnp.broadcast_to(bias, (side, 128))
+        par["live"][c + 1] = jnp.broadcast_to(jnp.where(live, KEEP, 0.0), (side, 128))
+        if c < 2:
+            corner = (t == side - 1) & (lane == side - 1)
+            par["pick"][c] = (pick + jnp.where(corner, 1.0, 0.0)).astype(BF16)
 
 
 def gather_gradients(total_ref, par, acc, kept):
@@ -278,37 +363,38 @@
     for c in range(2):
         pick = par["pick"][c]
         part = dot(acc["w_sp"][c, :, 0:rows].astype(BF16), pick).astype(BF16)
-        mix = mix + dot(par["pick"][2 + c], part)
+        mix = mix + dot_tn(pick, part)
     total_ref[:, base:] = jnp.zeros((width, total_ref.shape[1] - base), BF16)
     total_ref[0:rows, base : base + rows] = mix.astype(BF16)
     lines = []
     for name in LINES:
         v = jnp.sum(acc[name][...], axis=0, keepdims=True)
         lines += [v[:, i * width : (i + 1) * width] for i in range(v.shape[1] // width)]
-    lines.append(jnp.zeros((16 - len(lines), width), F32))
     more = [acc["w_in"][width : width + 1, i * width : (i + 1) * width] for i in range(wide // width)]
-    more.append(jnp.zeros((16 - len(more), width), F32))
+    more.append(jnp.zeros((32 - len(lines) - len(more), width), F32))
     total_ref[rows : rows + 32, base : base + width] = jnp.concatenate(lines + more, axis=0).astype(BF16)
 
 
-def layer_kernel(orders, spans, sizes, slot_count, groups, pair, cls_ref, *refs):
+def layer_kernel(orders, spans, sizes, slot_count, groups, quarter, lengths, pair, cls_ref, *refs):
     depth = len(orders[0])
     packed, refs = refs[:groups], refs[groups:]
-    par, refs = dict(zip(PAR, refs)), refs[len(PAR) :]
+    weights, w_sp_ref, vector_ref, *refs = refs[:2], *refs[2:]
     out_ref, back_ref, total_ref, parcel, *refs = refs
+    names = TABLES + LARGE + VECTORS
+    par, refs = {"w_sp": w_sp_ref} | dict(zip(names, refs)), refs[len(names) :]
     acc, refs = dict(zip(ACC, refs)), refs[len(ACC) :]
     scr, refs = dict(zip(SCR, refs)), refs[len(SCR) :]
     kept, refs = dict(zip(KEPT, refs)), refs[len(KEPT) :]
     first, *refs = refs
     rbufs, refs = refs[:depth], refs[depth:]
-    send_sem, recv_sem, in_send, in_recv, back_send, back_recv, own_sem = refs
+    send_sem, recv_sem, in_send, in_recv, back_send, back_recv, own_sem, load_sem = refs
     dp, patch = lax.axis_index("dp"), lax.axis_index("patch")
     core = patch & 1
 
     def peer(axis, bit):
         return (dp ^ bit, patch) if axis == "dp" else (dp, patch ^ bit)
 
-    peers = [peer("patch", 1), peer("patch", 3)] + [peer(a, b) for a, b in orders[0]]
+    peers = [peer("patch", 1), peer("patch", 3)] + [peer(a, mask) for a, bits in orders[0] for mask in combos(bits)]
     barrier = pltpu.get_barrier_semaphore()
     for other in peers:
         pl.semaphore_signal(barrier, inc=1, device_id=other, device_id_type=MESH)
@@ -333,11 +419,30 @@
             device_id=peer("patch", k), device_id_type=MESH,
         )
 
+    def give_back(begin, end):
+        @pl.loop(begin, end)
+        def _(j):
+            for k in range(groups - 1, -1, -1):
+                back(k, j).start()
+
+    stops = [slots * n // 6 for n in (0, *BACKS, 6)]
+
     @pl.loop(0, slots)
     def _(j):
         for k in range(groups - 1, -1, -1):
             inward(k, j).start()
 
+    loads = [pltpu.make_async_copy(weights[i], par[name], load_sem.at[i]) for i, name in enumerate(LARGE)]
+    for load in loads:
+        load.start()
+    line = 0
+    for name in VECTORS:
+        length = par[name].shape[1]
+        for begin in range(0, length, vector_ref.shape[1]):
+            stop = min(length, begin + vector_ref.shape[1])
+            par[name][:, begin:stop] = vector_ref[line : line + 1, 0 : stop - begin]
+            line += 1
+    fill_tables(par, quarter, slot_count, groups)
     for ref in acc.values():
         ref[...] = jnp.zeros_like(ref)
     rows = scr["xs"].shape[0]
@@ -347,11 +452,22 @@
     n = groups * slot_count
     for name in ("xs", "dys"):
         scr[name][rows - 16 : rows, :] = jnp.zeros((16, scr[name].shape[1]), F32)
+    for load in loads:
+        load.wait()
 
     @pl.loop(0, slots)
     def _(j):
         for k in range(groups):
             inward(k, j).wait()
+
+        @pl.when(j == slots - 2)
+        def _():
+            give_back(stops[0], stops[1])
+
+        @pl.when(j == slots - 1)
+        def _():
+            give_back(stops[1], stops[2])
+
         half_at = pl.ds(pl.multiple_of(lax.rem(j, pair) * rows, 16), rows)
         views = {name: ref.at[half_at] for name, ref in kept.items()}
         image_work(cls_ref[j], j, slot_count, patch, parcel, par, acc, scr | views)
@@ -368,9 +484,9 @@
     theirs = pl.multiple_of((1 - core) * half, 128)
     copies = []
 
-    def send(src, dst, step, i, other):
+    def send(src, dst, step, i, part, other):
         copy = pltpu.make_async_remote_copy(
-            src_ref=src, dst_ref=dst, send_sem=send_sem.at[step, i], recv_sem=recv_sem.at[step, i], device_id=other,
+            src_ref=src, dst_ref=dst, send_sem=send_sem.at[part, step, i], recv_sem=recv_sem.at[part, step, i], device_id=other,
             device_id_type=MESH,
         )
         copy.start()
@@ -383,72 +499,85 @@
     def shifted(base, i):
         return pl.ds(pl.multiple_of(base + spans[i][0], 128), spans[i][1])
 
-    def high(axis, bit):
-        return jnp.where(((dp if axis == "dp" else patch) & bit) != 0, 1, 0)
-
-    def give_back(begin, end):
-        @pl.loop(begin, end)
-        def _(j):
-            for k in range(groups - 1, -1, -1):
-                back(k, j).start()
+    def rank_in(axis, bits):
+        index = dp if axis == "dp" else patch
+        return sum(jnp.where((index & bit) != 0, 1 << n, 0) for n, bit in enumerate(bits))
+
+    def other_rank(axis, bits, mask):
+        index = (dp if axis == "dp" else patch) ^ mask
+        return sum(jnp.where((index & bit) != 0, 1 << n, 0) for n, bit in enumerate(bits))
+
+    def rows_at(begin, size):
+        return pl.ds(pl.multiple_of(begin, 16), size)
 
     state = [0] * pieces
     flying = [
-        send(total_ref.at[:, shifted(theirs, i)], first.at[:, cols(i)], 0, i, peer("patch", 1)) for i in range(pieces)
+        [send(total_ref.at[:, shifted(theirs, i)], first.at[:, cols(i)], 0, i, 0, peer("patch", 1))] for i in range(pieces)
     ]
-    early = slots * EARLY // 6
-    give_back(0, early)
+    give_back(stops[2], stops[3])
     for s in range(depth + 1):
+        if s == 2:
+            give_back(stops[3], stops[4])
         for i in range(pieces):
-            flying[i].wait_recv()
+            size = sizes[i][s]
+            for copy in flying[i]:
+                copy.wait_recv()
             lo = state[i]
-            if s > 0 and sizes[s - 1] == sizes[s]:
-                flying[i].wait_send()
-                copies[:] = [copy for copy in copies if copy is not flying[i]]
+            if s > 0 and sizes[i][s - 1] == size:
+                for copy in flying[i]:
+                    copy.wait_send()
+                copies[:] = [copy for copy in copies if all(copy is not old for old in flying[i])]
             got_ref = first if s == 0 else rbufs[s - 1]
-            unit = 32 if sizes[s] % 32 == 0 else 16
-
-            @pl.loop(0, sizes[s], step=unit)
-            def _(r, i=i, lo=lo, got_ref=got_ref, unit=unit):
-                at = pl.ds(pl.multiple_of(lo + r, 16), unit)
-                got = pl.ds(pl.multiple_of(r, 16), unit)
-                total_ref[at, shifted(mine, i)] = (
-                    total_ref[at, shifted(mine, i)].astype(F32) + got_ref[got, cols(i)].astype(F32)
-                ).astype(BF16)
+            unit = 32 if size % 32 == 0 else 16
+
+            @pl.loop(0, size, step=unit)
+            def _(r, i=i, lo=lo, got_ref=got_ref, unit=unit, size=size, parts=len(flying[i])):
+                at = rows_at(lo + r, unit)
+                value = total_ref[at, shifted(mine, i)].astype(F32)
+                for part in range(parts):
+                    value = value + got_ref[rows_at(part * size + r, unit), cols(i)].astype(F32)
+                total_ref[at, shifted(mine, i)] = value.astype(BF16)
 
             if s < depth:
-                axis, bit = orders[i][s]
-                keep = sizes[s + 1]
-                give = state[i]
-                if keep < sizes[s]:
-                    give = pl.multiple_of(state[i] + (1 - high(axis, bit)) * keep, 16)
-                    state[i] = pl.multiple_of(state[i] + high(axis, bit) * keep, 16)
-                flying[i] = send(
-                    total_ref.at[pl.ds(give, keep), shifted(mine, i)], rbufs[s].at[pl.ds(0, keep), cols(i)], s + 1, i,
-                    peer(axis, bit),
-                )
+                axis, bits = orders[i][s]
+                keep = sizes[i][s + 1]
+                base = state[i]
+                split = keep < size
+                if split:
+                    state[i] = base + rank_in(axis, bits) * keep
+                flying[i] = []
+                for part, mask in enumerate(combos(bits)):
+                    give = base + other_rank(axis, bits, mask) * keep if split else base
+                    flying[i].append(
+                        send(
+                            total_ref.at[rows_at(give, keep), shifted(mine, i)],
+                            rbufs[s].at[pl.ds(part * keep, keep), cols(i)], s + 1, i, part, peer(axis, mask),
+                        )
+                    )
     for i in range(pieces):
-        at = pl.ds(pl.multiple_of(state[i], 16), sizes[depth])
+        at = rows_at(state[i], sizes[i][depth])
         out_ref[at, shifted(mine, i)] = total_ref[at, shifted(mine, i)]
-    flying = [None] * pieces
+    flying = [[] for _ in range(pieces)]
     for s in range(depth, -1, -1):
-        if s == depth - 2:
-            give_back(early, slots)
+        if s == depth - 1:
+            give_back(stops[4], stops[5])
         for i in range(pieces):
-            if flying[i] is not None:
-                flying[i].wait_recv()
-                flying[i] = None
+            for copy in flying[i]:
+                copy.wait_recv()
+            flying[i] = []
             step = 2 * depth + 1 - s
             if s == 0:
                 where = out_ref.at[:, shifted(mine, i)]
-                flying[i] = send(where, where, step, i, peer("patch", 1))
-            elif sizes[s] < sizes[s - 1]:
-                axis, bit = orders[i][s - 1]
-                where = out_ref.at[pl.ds(pl.multiple_of(state[i], 16), sizes[s]), shifted(mine, i)]
-                flying[i] = send(where, where, step, i, peer(axis, bit))
-                state[i] = state[i] - high(axis, bit) * sizes[s]
+                flying[i] = [send(where, where, step, i, 0, peer("patch", 1))]
+            elif sizes[i][s] < sizes[i][s - 1]:
+                axis, bits = orders[i][s - 1]
+                where = out_ref.at[rows_at(state[i], sizes[i][s]), shifted(mine, i)]
+                for part, mask in enumerate(combos(bits)):
+                    flying[i].append(send(where, where, step, i, part, peer(axis, mask)))
+                state[i] = state[i] - rank_in(axis, bits) * sizes[i][s]
     for i in range(pieces):
-        flying[i].wait_recv()
+        for copy in flying[i]:
+            copy.wait_recv()
 
     @pl.loop(0, slots)
     def _(j):
@@ -459,9 +588,9 @@
         copy.wait_send()
 
 
-def call_layer(cls, packed, par, dp, groups, slot_count, pieces):
+def call_layer(cls, packed, w_in, w_out, w_pad, vectors, lengths, dp, groups, slot_count, quarter, pieces):
     slots, stage_rows, width = packed[0].shape
-    wide, half, side = par["w_in"].shape[1], par["w_out"].shape[0], par["wsp"].shape[1]
+    wide, half, side = w_in.shape[1], w_out.shape[0], w_pad.shape[0]
     span = up(side, 128)
     pair = 2 if slots % 2 == 0 else 1
     columns = wide + half + width
@@ -470,7 +599,11 @@
     starts = np.cumsum([0] + [w * 128 for _, w in pieces])
     spans = [(int(starts[i]), w * 128) for i, (_, w) in enumerate(pieces)]
     depth = len(orders[0])
-    sizes = plan_sizes(depth, width)
+    sizes = [plan_sizes(order, width) for order in orders]
+    room_for = [
+        max(len(combos(order[s][1])) * size[s + 1] for order, size in zip(orders, sizes)) for s in range(depth)
+    ]
+    fan = max(len(combos(bits)) for _, bits in orders[0])
     vmem = pl.BlockSpec(memory_space=pltpu.VMEM)
     far = pl.BlockSpec(memory_space=pl.ANY)
     acc = {
@@ -484,27 +617,30 @@
     }
     room = up(pair * side, 256)
     return pl.pallas_call(
-        functools.partial(layer_kernel, orders, spans, sizes, slot_count, groups, pair),
+        functools.partial(layer_kernel, orders, spans, sizes, slot_count, groups, quarter, lengths, pair),
         out_shape=[
             jax.ShapeDtypeStruct((width, columns), BF16),
             jax.ShapeDtypeStruct((slots * groups, stage_rows, width), BF16),
         ],
-        in_specs=[pl.BlockSpec(memory_space=pltpu.SMEM)] + [far] * groups + [vmem] * len(PAR),
+        in_specs=[pl.BlockSpec(memory_space=pltpu.SMEM)] + [far] * groups + [far, far, vmem, vmem],
         out_specs=[vmem, far],
         scratch_shapes=[pltpu.VMEM((width, columns), BF16), pltpu.VMEM((groups, slots, stage_rows, width), BF16)]
+        + [pltpu.VMEM((n, side, m), t) for n, m, t in ((4, side, BF16), (4, side, BF16), (4, 128, F32), (4, 128, F32), (2, side, BF16))]
+        + [pltpu.VMEM(w_in.shape, BF16), pltpu.VMEM(w_out.shape, BF16)]
+        + [pltpu.VMEM((1, n), F32) for n in lengths]
         + [pltpu.VMEM(acc[name], F32) for name in ACC]
         + [pltpu.VMEM(*scr[name]) for name in SCR]
         + [pltpu.VMEM((room, n), BF16) for n in (width, width, half, wide)]
         + [pltpu.VMEM((width, columns // 2), BF16)]
-        + [pltpu.VMEM((size, columns // 2), BF16) for size in sizes[1:]]
-        + [pltpu.SemaphoreType.DMA((2 * depth + 2, len(pieces)))] * 2
+        + [pltpu.VMEM((size, columns // 2), BF16) for size in room_for]
+        + [pltpu.SemaphoreType.DMA((fan, 2 * depth + 2, len(pieces)))] * 2
         + [pltpu.SemaphoreType.DMA((groups, slots))] * 4
-        + [pltpu.SemaphoreType.DMA((2, slots))],
+        + [pltpu.SemaphoreType.DMA((2, slots)), pltpu.SemaphoreType.DMA((2,))],
         compiler_params=pltpu.CompilerParams(
             collective_id=1, has_side_effects=True, vmem_limit_bytes=64 * 1024 * 1024 - 65536
         ),
         name="layer",
-    )(cls, *packed, *[par[name] for name in PAR])
+    )(cls, *packed, w_in, w_out, w_pad, vectors)
 
 
 def local(images, cotangent, res_class, skip, ln_gain, ln_bias, w_in, b_in, gate_gain, gate_bias, w_spatial, b_spatial, w_out, b_out):
@@ -541,78 +677,50 @@
         functools.partial(pack_kernel, slot_count, groups),
         out_shape=[jax.ShapeDtypeStruct((slots, stage_rows, width), BF16)] * groups,
         in_specs=[smem, smem, whole, whole],
-        out_specs=[whole] * groups,
-        scratch_shapes=[pltpu.VMEM(planes, F32), pltpu.VMEM(planes, F32), pltpu.VMEM((stage_rows, width), F32)],
-        compiler_params=pltpu.CompilerParams(vmem_limit_bytes=40 * 1024 * 1024),
+        out_specs=[pl.BlockSpec(memory_space=pltpu.HBM)] * groups,
+        scratch_shapes=[pltpu.VMEM((groups, slots, stage_rows, width), BF16), pltpu.VMEM(planes, F32), pltpu.VMEM(planes, F32)]
+        + [pltpu.VMEM((stage_rows, width), F32), pltpu.SemaphoreType.DMA((groups, slots))],
+        compiler_params=pltpu.CompilerParams(vmem_limit_bytes=62 * 1024 * 1024),
         name="pack",
     )(me1, order, img_t, cot_t)
 
-    live, where = [], []
-    at = jnp.arange(side, dtype=jnp.int32)
-    place, within = at // slot_count, at % slot_count
-    for q in quarter:
-        live.append((within < q) & (at < patches))
-        where.append(jnp.where(live[-1], place * q + within, -1))
-    picks = [(w[:, None] == at[None, :]).astype(BF16) for w in where]
     w_pad = jnp.pad(w_spatial, ((0, side - patches),) * 2)
-    b_pad = jnp.pad(b_spatial, (0, side - patches))
-    spread = [jnp.zeros((side, side), BF16)]
-    bias = [jnp.zeros((side,), F32)]
-    for c, pick in enumerate(picks):
-        if c < 2:
-            moved = jnp.einsum("ta,ab->tb", pick, w_pad, preferred_element_type=F32).astype(BF16)
-            spread.append(jnp.einsum("tb,sb->ts", moved, pick, preferred_element_type=F32).astype(BF16))
-            bias.append(jnp.sum(jnp.where(where[c][:, None] == at[None, :], b_pad[None, :], 0.0), axis=1))
-        else:
-            spread.append(w_pad)
-            bias.append(b_pad)
-    wsp = jnp.stack(spread)
-    wsp_t = jnp.swapaxes(wsp, 1, 2)
-    bsp = jnp.stack([jnp.broadcast_to(v[:, None], (side, 128)) for v in bias])
-    keep = jnp.stack([jnp.zeros((side, 128), F32)] + [jnp.broadcast_to(jnp.where(v, KEEP, 0.0)[:, None], (side, 128)) for v in live])
-    corner = ((at[:, None] == side - 1) & (at[None, :] == side - 1)).astype(BF16)
-    lift = [pick + corner for pick in picks[:2]]
-    pick = jnp.stack(lift + [v.T for v in lift])
-    par = {
-        "ln_gain": ln_gain[None, :], "ln_bias": ln_bias[None, :], "w_in": w_in, "b_in": b_in[None, :],
-        "gate_gain": gate_gain[None, :], "gate_bias": gate_bias[None, :], "wsp": wsp, "wsp_t": wsp_t, "bsp": bsp, "live": keep, "pick": pick,
-        "w_out": w_out, "b_out": b_out[None, :],
-    }
-    summed, backs = call_layer(cls, packed, par, dp, groups, slot_count, PIECES)
-    out_t, grad_t = pl.pallas_call(
-        functools.partial(unpack_kernel, slot_count, quarter),
-        out_shape=[jax.ShapeDtypeStruct((slot_count, count, width), BF16), jax.ShapeDtypeStruct((slot_count, count, width), F32)],
-        in_specs=[smem, smem] + [whole] * 3,
-        out_specs=[whole, whole],
-        scratch_shapes=[pltpu.VMEM(planes, F32), pltpu.VMEM(planes, F32), pltpu.VMEM((stage_rows, width), F32)],
-        compiler_params=pltpu.CompilerParams(vmem_limit_bytes=40 * 1024 * 1024),
-        name="unpack",
-    )(rank, key, img_t, cot_t, backs)
-    output = jnp.swapaxes(out_t, 0, 1)
-    grad_images = jnp.swapaxes(grad_t, 0, 1)
-
-    cut = 2 * CT
-    first, last = wide // cut, (wide + half) // cut
-    g_w_in, g_w_out = pl.pallas_call(
-        functools.partial(widen_kernel, first),
-        out_shape=[jax.ShapeDtypeStruct((width, wide), F32), jax.ShapeDtypeStruct((half, width), F32)],
-        grid=(last,),
-        in_specs=[pl.BlockSpec((width, cut), lambda t: (0, t))],
+    vectors = (b_in, gate_gain, gate_bias, ln_gain, ln_bias, b_out, b_spatial)
+    filled = sum(v.shape[0] for v in vectors)
+    table = jnp.concatenate([*vectors, jnp.zeros((up(filled, 8 * width) - filled,), F32)]).reshape(-1, width)
+    lengths = tuple(side if v is b_spatial else v.shape[0] for v in vectors)
+    summed, backs = call_layer(cls, packed, w_in, w_out, w_pad, table, lengths, dp, groups, slot_count, quarter, PIECES)
+    cut = 512
+    inner, outer = wide // cut, half // cut
+    far = pl.BlockSpec(memory_space=pl.ANY)
+    rowed = [jax.ShapeDtypeStruct((n,), F32) for n in (half, half, width, width, width, wide)]
+    swapped = (slot_count, count, width)
+    results = pl.pallas_call(
+        functools.partial(finish_kernel, slot_count, quarter, wide, half),
+        out_shape=[
+            jax.ShapeDtypeStruct((width, wide), F32), jax.ShapeDtypeStruct((half, width), F32),
+            jax.ShapeDtypeStruct((patches, patches), F32), jax.ShapeDtypeStruct((patches,), F32),
+            *rowed, jax.ShapeDtypeStruct(swapped, BF16), jax.ShapeDtypeStruct(swapped, F32),
+        ],
+        grid=(1 + inner + outer,),
+        in_specs=[smem, smem, far, far, far]
+        + [pl.BlockSpec((width, cut), lambda t: (0, jnp.where(t == 0, inner + outer, t - 1)))],
         out_specs=[
-            pl.BlockSpec((width, cut), lambda t: (0, jnp.minimum(t, first - 1))),
-            pl.BlockSpec((cut, width), lambda t: (jnp.maximum(t - first, 0), 0)),
-        ],
-        name="widen",
-    )(summed)
-    base = wide + half
-    small = summed[0 : side + 32, base:].astype(F32)
-    lines = small[side : side + 16].reshape(-1)
-    ends = np.cumsum([0, half, half, width, width, width])
-    g_gate_gain, g_gate_bias, g_ln_gain, g_ln_bias, g_b_out = [lines[ends[i] : ends[i + 1]] for i in range(5)]
-    g_b_in = small[side + 16 : side + 32].reshape(-1)[:wide]
+            pl.BlockSpec((width, cut), lambda t: (0, jnp.clip(t - 1, 0, inner - 1))),
+            pl.BlockSpec((cut, width), lambda t: (jnp.maximum(t - 1 - inner, 0), 0)),
+        ]
+        + [whole] * 8
+        + [far, far],
+        scratch_shapes=[pltpu.VMEM(planes, F32), pltpu.VMEM(planes, F32), pltpu.VMEM((stage_rows, width), F32)]
+        + [pltpu.VMEM(swapped, BF16), pltpu.VMEM(swapped, F32), pltpu.VMEM(swapped, BF16), pltpu.VMEM(swapped, BF16)]
+        + [pltpu.VMEM(backs.shape, BF16), pltpu.SemaphoreType.DMA((5,))],
+        compiler_params=pltpu.CompilerParams(vmem_limit_bytes=56 * 1024 * 1024),
+        name="finish",
+    )(rank, key, img_t, cot_t, backs, summed)
+    g_w_in, g_w_out, g_w_sp, g_b_sp, g_gate_gain, g_gate_bias, g_ln_gain, g_ln_bias, g_b_out, g_b_in, out_t, grad_t = results
     return (
-        output, grad_images, g_ln_gain, g_ln_bias, g_w_in, g_b_in, g_gate_gain, g_gate_bias,
-        small[:patches, :patches], small[:patches, side - 1], g_w_out, g_b_out,
+        jnp.swapaxes(out_t, 0, 1), jnp.swapaxes(grad_t, 0, 1), g_ln_gain, g_ln_bias, g_w_in, g_b_in,
+        g_gate_gain, g_gate_bias, g_w_sp, g_b_sp, g_w_out, g_b_out,
     )
 
 

time: 222 us -> 170 us (0.77)
  Pallas kernels: 191 us -> 164 us
  local copies, waits for them, and re-layouts: 20.2 us -> 3.14 us
  other arithmetic: 8.6 us -> 2.18 us
    pallas_call x1, Pallas kernels: 172 us -> 142 us  [call_layer(): pl.pallas_call(functools.partial(layer_kernel, orders, spans, sizes, slot...]
    unnamed x29 -> x4, local copies, waits for them, and re-layouts: 10.8 us -> 0.01 us
    slice x8 -> x0, local copies, waits for them, and re-layouts: 4.05 us -> none  [the longest x4 1.81 us: local(): lines[ends[i]:ends[i + 1]]]
    another operation x3 -> x0, other arithmetic: 3.84 us -> none  [the longest x1 1.31 us: local(): wsp = jnp.stack(spread)]
    broadcast_in_dim x2 -> x1, local copies, waits for them, and re-layouts: 2.59 us -> 0.01 us  [local(): jnp.zeros((up(filled, 8 * width) - filled,), F32)]
    pallas_call x1, Pallas kernels: 3.38 us -> 5.93 us  [local(): pl.pallas_call(functools.partial(pack_kernel, slot_count, groups), out_sh...]
    pallas_call x2 -> x1, Pallas kernels: 15.5 us -> 16.3 us  [local(): pl.pallas_call(functools.partial(finish_kernel, slot_count, quarter, wide...]
where the time goes in v3:
time: 170 us
  Pallas kernels  164 us (96%)
  local copies, waits for them, and re-layouts  3.14 us (2%)
  other arithmetic  2.18 us (1%)
    pallas_call x1, Pallas kernels, call_layer(): pl.pallas_call(functools.partial(layer_kernel, orders, spans, sizes, slot...  142 us
    pallas_call x1, Pallas kernels, local(): pl.pallas_call(functools.partial(finish_kernel, slot_count, quarter, wide...  16.3 us
    pallas_call x1, Pallas kernels, local(): pl.pallas_call(functools.partial(pack_kernel, slot_count, groups), out_sh...  5.93 us

profile of v3, /device:TPU:1, one launch (start us, length us, event | category | flops | bytes accessed | tf_op | source)
XLA Modules:
  0.0 170.1 jit_solution(13308986797793125663)
XLA Ops:
  0.7 0.7 compare_select_fusion.1.key_ref
  1.3 0.0 copy-start
  1.3 0.2 convert_reduce_fusion.rank_ref
  1.5 0.0 copy-start.1
  1.5 0.7 select_reduce_fusion.1.cls_ref
  2.2 0.6 select_reduce_fusion.order_ref
  2.8 0.0 copy-done
  2.8 0.0 copy-done.1
  2.9 0.9 concatenate.3
  3.7 0.6 reshape.48.refs_7_
  4.3 1.7 pad.4.refs_6_
  6.0 5.9 %pack.1 = (bf16[6,176,512]{2,1,0:T(8,128)(2,1)}, bf16[6,176,512]{2,1,0:T(8,128)(2,1)}, bf16[6,176,512]{2,1,0:T(8,128)(2,1)}, bf16[6,176,512]{2,1,0:T(8,128)(2,1)}) custom-call(s32[1]{0:T(128)} %bitcast.2.me_ref, s32[24]{0:T(128)} %select_reduce_fusion.order_ref, bf16[81,24,512]{2,1,0:T(8,128)(2,1)} %bitcast.5, bf16[81,24,512]{2,1,0:T(8,128)(2,1)} %bitcast.7), custom_call_target="tpu_custom_call" | custom-call | tf_op jit(solution)/shard_map/pack/pallas_call | solution.py:676
  11.9 141.6 %layer.1 = (bf16[512,5120]{1,0:T(8,128)(2,1)}, bf16[24,176,512]{2,1,0:T(8,128)(2,1)}) custom-call(s32[6]{0:T(128)} %select_reduce_fusion.1.cls_ref, bf16[6,176,512]{2,1,0:T(8,128)(2,1)} %get-tuple-element.30.refs_0_, bf16[6,176,512]{2,1,0:T(8,128)(2,1)} %get-tuple-element.31.refs_1_, bf16[6,176,512]{2,1,0:T(8,128)(2,1)} %get-tuple-element.32.refs_2_, ...), custom_call_target="tpu_custom_call" | custom-call | tf_op jit(solution)/shard_map/layer/pallas_call | solution.py:619
  153.6 16.3 %finish.1 = (f32[512,3072]{1,0:T(8,128)}, f32[1536,512]{1,0:T(8,128)}, f32[324,324]{1,0:T(8,128)}, f32[324]{0:T(512)}, f32[1536]{0:T(1024)}, /*index=5*/f32[1536...) custom-call(s32[24]{0:T(128)} %copy-done.1, ...), custom_call_target="tpu_custom_call" | custom-call | tf_op jit(solution)/shard_map/finish/pallas_call | solution.py:698
  (2 shorter events, 0.0 us)
Async XLA Ops:
  1.3 1.5 copy-start
  1.5 1.3 copy-start.1

commit v4 on v3

--- a/solution.py
+++ b/solution.py
@@ -15,7 +15,8 @@
 BF16 = jnp.bfloat16
 CT = 256
 BACKS = (4, 4, 4, 5)
-PIECES = (("c", 1), ("d", 2), ("b", 2)) * 4
+PAIR = 3
+PIECES = (("c", 1), ("d", 2), ("b", 2)) * 3 + (("c", 1), ("d", 1), ("b", 1), ("d", 1), ("b", 1))
 KEEP = np.float32(1.0) / np.float32(0.9)
 GELU_C = np.float32(np.sqrt(2.0 / np.pi))
 GELU_K = np.float32(0.044715)
@@ -97,7 +98,7 @@
     t = pl.program_id(0)
     small, first = 0, 1
     last = first + (wide + half) // cut
-    part = -(-count // (last - 4))
+    part = -(-count // 3)
     copies = [pltpu.make_async_copy(out, out_ref, sem.at[0]), pltpu.make_async_copy(grad, grad_ref, sem.at[1])]
     loads = [
         pltpu.make_async_copy(a, b, sem.at[2 + i])
@@ -120,7 +121,7 @@
                 ref[n * width : (n + 1) * width] = block[at, :]
                 at += 1
 
-    @pl.when(t == first)
+    @pl.when(t == first + 1)
     def _():
         for load in loads:
             load.wait()
@@ -140,7 +141,7 @@
     def _():
         out_w_ref[...] = src_ref[...].astype(F32).T
 
-    @pl.loop(jnp.clip((t - 2) * part, 0, count), jnp.clip((t - 1) * part, 0, count))
+    @pl.loop(jnp.clip((t - 3) * part, 0, count), jnp.clip((t - 2) * part, 0, count))
     def _(i):
         key = key_ref[i]
         for c, q in enumerate(quarter):
@@ -154,7 +155,7 @@
                     xf[b, at, :] = xf[b, at, :] + stage[0:q, cols]
                     yf[b, at, :] = yf[b, at, :] + stage[slot_count : slot_count + q, cols]
 
-    @pl.when(t == last - 2)
+    @pl.when(t == first + 5)
     def _():
         @pl.loop(0, slot_count, unroll=9)
         def _(r):
@@ -318,9 +319,10 @@
 
 
 def fill_tables(par, quarter, slot_count, groups):
-    side = par["w_sp"].shape[0]
+    side = par["wsp"].shape[1]
     t = lax.broadcasted_iota(jnp.int32, (side, 1), 0)
-    lane = lax.broadcasted_iota(jnp.int32, (1, side), 1)
+    lane = lax.broadcasted_iota(jnp.int32, (1, slot_count * groups), 1)
+    lanes = lax.broadcasted_iota(jnp.int32, (1, side), 1)
     place = sum(jnp.where(t >= slot_count * g, 1, 0) for g in range(1, groups))
     within = t - slot_count * place
     w = par["w_sp"][...]
@@ -329,16 +331,16 @@
     for c, q in enumerate(quarter):
         live = (within < q) & (t < slot_count * groups)
         hit = live & (place * q + within == lane)
-        pick = jnp.where(hit, 1.0, 0.0)
-        low = pick.astype(BF16)
+        low = jnp.where(hit, 1.0, 0.0).astype(BF16)
         par["wsp"][c + 1] = dot_nt(dot(low, w).astype(BF16), low).astype(BF16)
         par["wsp_t"][c + 1] = dot_nt(dot_nt(low, w).astype(BF16), low).astype(BF16)
         bias = jnp.sum(jnp.where(hit, par["b_sp"][...], 0.0), axis=-1, keepdims=True)
         par["bsp"][c + 1] = jnp.broadcast_to(bias, (side, 128))
         par["live"][c + 1] = jnp.broadcast_to(jnp.where(live, KEEP, 0.0), (side, 128))
         if c < 2:
-            corner = (t == side - 1) & (lane == side - 1)
-            par["pick"][c] = (pick + jnp.where(corner, 1.0, 0.0)).astype(BF16)
+            corner = (t == side - 1) & (lanes == side - 1)
+            chosen = (live & (place * q + within == lanes)) | corner
+            par["pick"][c] = jnp.where(chosen, 1.0, 0.0).astype(BF16)
 
 
 def gather_gradients(total_ref, par, acc, kept):
@@ -375,10 +377,10 @@
     total_ref[rows : rows + 32, base : base + width] = jnp.concatenate(lines + more, axis=0).astype(BF16)
 
 
-def layer_kernel(orders, spans, sizes, slot_count, groups, quarter, lengths, pair, cls_ref, *refs):
+def layer_kernel(orders, spans, sizes, slot_count, groups, quarter, pair, cls_ref, *refs):
     depth = len(orders[0])
     packed, refs = refs[:groups], refs[groups:]
-    weights, w_sp_ref, vector_ref, *refs = refs[:2], *refs[2:]
+    weights, w_sp_ref, given, refs = refs[:2], refs[2], refs[3 : 3 + len(VECTORS)], refs[3 + len(VECTORS) :]
     out_ref, back_ref, total_ref, parcel, *refs = refs
     names = TABLES + LARGE + VECTORS
     par, refs = {"w_sp": w_sp_ref} | dict(zip(names, refs)), refs[len(names) :]
@@ -435,13 +437,8 @@
     loads = [pltpu.make_async_copy(weights[i], par[name], load_sem.at[i]) for i, name in enumerate(LARGE)]
     for load in loads:
         load.start()
-    line = 0
-    for name in VECTORS:
-        length = par[name].shape[1]
-        for begin in range(0, length, vector_ref.shape[1]):
-            stop = min(length, begin + vector_ref.shape[1])
-            par[name][:, begin:stop] = vector_ref[line : line + 1, 0 : stop - begin]
-            line += 1
+    for name, ref in zip(VECTORS, given):
+        par[name][...] = ref[...].reshape(1, ref.shape[0])
     fill_tables(par, quarter, slot_count, groups)
     for ref in acc.values():
         ref[...] = jnp.zeros_like(ref)
@@ -588,11 +585,11 @@
         copy.wait_send()
 
 
-def call_layer(cls, packed, w_in, w_out, w_pad, vectors, lengths, dp, groups, slot_count, quarter, pieces):
+def call_layer(cls, packed, w_in, w_out, w_spatial, vectors, dp, groups, slot_count, quarter, pieces):
     slots, stage_rows, width = packed[0].shape
-    wide, half, side = w_in.shape[1], w_out.shape[0], w_pad.shape[0]
+    wide, half, side = w_in.shape[1], w_out.shape[0], up(w_spatial.shape[0], 16)
     span = up(side, 128)
-    pair = 2 if slots % 2 == 0 else 1
+    pair = PAIR if slots % PAIR == 0 else 1
     columns = wide + half + width
     table = reduce_orders(dp)
     orders = [table[name] for name, _ in pieces]
@@ -617,17 +614,17 @@
     }
     room = up(pair * side, 256)
     return pl.pallas_call(
-        functools.partial(layer_kernel, orders, spans, sizes, slot_count, groups, quarter, lengths, pair),
+        functools.partial(layer_kernel, orders, spans, sizes, slot_count, groups, quarter, pair),
         out_shape=[
             jax.ShapeDtypeStruct((width, columns), BF16),
             jax.ShapeDtypeStruct((slots * groups, stage_rows, width), BF16),
         ],
-        in_specs=[pl.BlockSpec(memory_space=pltpu.SMEM)] + [far] * groups + [far, far, vmem, vmem],
+        in_specs=[pl.BlockSpec(memory_space=pltpu.SMEM)] + [far] * groups + [far, far, vmem] + [vmem] * len(vectors),
         out_specs=[vmem, far],
         scratch_shapes=[pltpu.VMEM((width, columns), BF16), pltpu.VMEM((groups, slots, stage_rows, width), BF16)]
         + [pltpu.VMEM((n, side, m), t) for n, m, t in ((4, side, BF16), (4, side, BF16), (4, 128, F32), (4, 128, F32), (2, side, BF16))]
         + [pltpu.VMEM(w_in.shape, BF16), pltpu.VMEM(w_out.shape, BF16)]
-        + [pltpu.VMEM((1, n), F32) for n in lengths]
+        + [pltpu.VMEM((1, v.shape[0]), F32) for v in vectors]
         + [pltpu.VMEM(acc[name], F32) for name in ACC]
         + [pltpu.VMEM(*scr[name]) for name in SCR]
         + [pltpu.VMEM((room, n), BF16) for n in (width, width, half, wide)]
@@ -640,7 +637,7 @@
             collective_id=1, has_side_effects=True, vmem_limit_bytes=64 * 1024 * 1024 - 65536
         ),
         name="layer",
-    )(cls, *packed, w_in, w_out, w_pad, vectors)
+    )(cls, *packed, w_in, w_out, w_spatial, *vectors)
 
 
 def local(images, cotangent, res_class, skip, ln_gain, ln_bias, w_in, b_in, gate_gain, gate_bias, w_spatial, b_spatial, w_out, b_out):
@@ -653,7 +650,6 @@
     quarter = tuple(side * side // groups for side in SIDES)
     patches = groups * slot_count
     side = up(patches, 16)
-    span = up(patches, 128)
     stage_rows = up(2 * slot_count, 16)
     me = lax.axis_index("patch").astype(jnp.int32)
 
@@ -684,12 +680,8 @@
         name="pack",
     )(me1, order, img_t, cot_t)
 
-    w_pad = jnp.pad(w_spatial, ((0, side - patches),) * 2)
     vectors = (b_in, gate_gain, gate_bias, ln_gain, ln_bias, b_out, b_spatial)
-    filled = sum(v.shape[0] for v in vectors)
-    table = jnp.concatenate([*vectors, jnp.zeros((up(filled, 8 * width) - filled,), F32)]).reshape(-1, width)
-    lengths = tuple(side if v is b_spatial else v.shape[0] for v in vectors)
-    summed, backs = call_layer(cls, packed, w_in, w_out, w_pad, table, lengths, dp, groups, slot_count, quarter, PIECES)
+    summed, backs = call_layer(cls, packed, w_in, w_out, w_spatial, vectors, dp, groups, slot_count, quarter, PIECES)
     cut = 512
     inner, outer = wide // cut, half // cut
     far = pl.BlockSpec(memory_space=pl.ANY)

time: 170 us -> 164 us (0.965)
  Pallas kernels: 164 us -> 160 us
  local copies, waits for them, and re-layouts: 3.14 us -> 0.38 us
    pallas_call x1, Pallas kernels: 142 us -> 139 us  [call_layer(): pl.pallas_call(functools.partial(layer_kernel, orders, spans, sizes, slot...]
    pallas_call x1, Pallas kernels: 16.3 us -> 14.6 us  [local(): pl.pallas_call(functools.partial(finish_kernel, slot_count, quarter, wide...]
where the time goes in v4:
time: 164 us; the launch traced here: 163 us
  Pallas kernels  160 us (98%)
  other arithmetic  2.18 us (1%)
    pallas_call x1, Pallas kernels, call_layer(): pl.pallas_call(functools.partial(layer_kernel, orders, spans, sizes, slot...  139 us
    pallas_call x1, Pallas kernels, local(): pl.pallas_call(functools.partial(finish_kernel, slot_count, quarter, wide...  14.6 us
    pallas_call x1, Pallas kernels, local(): pl.pallas_call(functools.partial(pack_kernel, slot_count, groups), out_sh...  5.94 us

profile of v4, /device:TPU:1, one launch (start us, length us, event | category | flops | bytes accessed | tf_op | source)
XLA Modules:
  0.0 163.4 jit_solution(14295866911871815855)
XLA Ops:
  0.7 0.7 compare_select_fusion.1.key_ref
  1.3 0.0 copy-start
  1.3 0.2 convert_reduce_fusion.rank_ref
  1.5 0.4 copy-done
  1.9 0.0 copy-start.1
  1.9 0.7 select_reduce_fusion.1.cls_ref
  2.6 0.0 copy-done.1
  2.6 0.6 select_reduce_fusion.order_ref
  3.2 5.9 %pack.1 = (bf16[6,176,512]{2,1,0:T(8,128)(2,1)}, bf16[6,176,512]{2,1,0:T(8,128)(2,1)}, bf16[6,176,512]{2,1,0:T(8,128)(2,1)}, bf16[6,176,512]{2,1,0:T(8,128)(2,1)}) custom-call(s32[1]{0:T(128)} %bitcast.2.me_ref, s32[24]{0:T(128)} %select_reduce_fusion.order_ref, bf16[81,24,512]{2,1,0:T(8,128)(2,1)} %bitcast.5, bf16[81,24,512]{2,1,0:T(8,128)(2,1)} %bitcast.7), custom_call_target="tpu_custom_call" | custom-call | tf_op jit(solution)/shard_map/pack/pallas_call | solution.py:672
  9.2 139.4 %layer.1 = (bf16[512,5120]{1,0:T(8,128)(2,1)}, bf16[24,176,512]{2,1,0:T(8,128)(2,1)}) custom-call(s32[6]{0:T(128)} %select_reduce_fusion.1.cls_ref, bf16[6,176,512]{2,1,0:T(8,128)(2,1)} %get-tuple-element.30.refs_0_, bf16[6,176,512]{2,1,0:T(8,128)(2,1)} %get-tuple-element.31.refs_1_, bf16[6,176,512]{2,1,0:T(8,128)(2,1)} %get-tuple-element.32.refs_2_, ...), custom_call_target="tpu_custom_call" | custom-call | tf_op jit(solution)/shard_map/layer/pallas_call | solution.py:616
  148.6 14.6 %finish.1 = (f32[512,3072]{1,0:T(8,128)}, f32[1536,512]{1,0:T(8,128)}, f32[324,324]{1,0:T(8,128)}, f32[324]{0:T(512)}, f32[1536]{0:T(1024)}, /*index=5*/f32[1536...) custom-call(s32[24]{0:T(128)} %copy-done.1, ...), custom_call_target="tpu_custom_call" | custom-call | tf_op jit(solution)/shard_map/finish/pallas_call | solution.py:690
  (1 shorter events, 0.0 us)
Async XLA Ops:
  1.3 0.6 copy-start
  1.9 0.7 copy-start.1

commit v5 on v4

--- a/solution.py
+++ b/solution.py
@@ -668,7 +668,7 @@
     smem = pl.BlockSpec(memory_space=pltpu.SMEM)
     img_t = jnp.swapaxes(images, 0, 1)
     cot_t = jnp.swapaxes(cotangent, 0, 1)
-    planes = (width // 128, slot_count * count, 128)
+    planes = (width // 128, (up(slot_count, 8) + 1) * count, 128)
     packed = pl.pallas_call(
         functools.partial(pack_kernel, slot_count, groups),
         out_shape=[jax.ShapeDtypeStruct((slots, stage_rows, width), BF16)] * groups,

time: 164 us -> 164 us (level)
  no operation moved by 1% of the time
where the time goes in v5:
time: 164 us; the launch traced here: 163 us
  Pallas kernels  160 us (98%)
  other arithmetic  2.18 us (1%)
    pallas_call x1, Pallas kernels, call_layer(): pl.pallas_call(functools.partial(layer_kernel, orders, spans, sizes, slot...  139 us
    pallas_call x1, Pallas kernels, local(): pl.pallas_call(functools.partial(finish_kernel, slot_count, quarter, wide...  14.9 us
    pallas_call x1, Pallas kernels, local(): pl.pallas_call(functools.partial(pack_kernel, slot_count, groups), out_sh...  5.93 us

profile of v5, /device:TPU:1, one launch (start us, length us, event | category | flops | bytes accessed | tf_op | source)
XLA Modules:
  0.0 163.4 jit_solution(4996820286410625129)
XLA Ops:
  0.7 0.7 compare_select_fusion.1.key_ref
  1.3 0.0 copy-start
  1.3 0.2 convert_reduce_fusion.rank_ref
  1.5 0.4 copy-done
  1.9 0.0 copy-start.1
  1.9 0.7 select_reduce_fusion.1.cls_ref
  2.6 0.0 copy-done.1
  2.6 0.6 select_reduce_fusion.order_ref
  3.2 5.9 %pack.1 = (bf16[6,176,512]{2,1,0:T(8,128)(2,1)}, bf16[6,176,512]{2,1,0:T(8,128)(2,1)}, bf16[6,176,512]{2,1,0:T(8,128)(2,1)}, bf16[6,176,512]{2,1,0:T(8,128)(2,1)}) custom-call(s32[1]{0:T(128)} %bitcast.2.me_ref, s32[24]{0:T(128)} %select_reduce_fusion.order_ref, bf16[81,24,512]{2,1,0:T(8,128)(2,1)} %bitcast.5, bf16[81,24,512]{2,1,0:T(8,128)(2,1)} %bitcast.7), custom_call_target="tpu_custom_call" | custom-call | tf_op jit(solution)/shard_map/pack/pallas_call | solution.py:672
  9.2 139.2 %layer.1 = (bf16[512,5120]{1,0:T(8,128)(2,1)}, bf16[24,176,512]{2,1,0:T(8,128)(2,1)}) custom-call(s32[6]{0:T(128)} %select_reduce_fusion.1.cls_ref, bf16[6,176,512]{2,1,0:T(8,128)(2,1)} %get-tuple-element.30.refs_0_, bf16[6,176,512]{2,1,0:T(8,128)(2,1)} %get-tuple-element.31.refs_1_, bf16[6,176,512]{2,1,0:T(8,128)(2,1)} %get-tuple-element.32.refs_2_, ...), custom_call_target="tpu_custom_call" | custom-call | tf_op jit(solution)/shard_map/layer/pallas_call | solution.py:616
  148.4 14.9 %finish.1 = (f32[512,3072]{1,0:T(8,128)}, f32[1536,512]{1,0:T(8,128)}, f32[324,324]{1,0:T(8,128)}, f32[324]{0:T(512)}, f32[1536]{0:T(1024)}, /*index=5*/f32[1536...) custom-call(s32[24]{0:T(128)} %copy-done.1, ...), custom_call_target="tpu_custom_call" | custom-call | tf_op jit(solution)/shard_map/finish/pallas_call | solution.py:690
  (1 shorter events, 0.0 us)
Async XLA Ops:
  1.3 0.6 copy-start
  1.9 0.7 copy-start.1
